TPU v7x, 256 devices: a whole 4x4x8 slice. The times are simulated.
256 devices in a mesh: lon: 16 (over z, y_hi), lat: 16 (over x, y_lo, core).
Axes of the slice: x: 4, y: 4 (y_hi: 2, y_lo: 2; y = y_hi * 2 + y_lo), z: 8, core: 2. Of those that a mesh axis runs over, the one named last changes fastest.
Arguments:
- grid: bfloat16 [8, 96, 192, 192], P(None, 'lat', 'lon'), may hold values from -24 to 24
- gains: float32 [2, 2, 192], replicated, may hold values from 0.1 to 1.9
- w_qkv: bfloat16 [2, 192, 576], replicated, may hold values from -1 to 1
- w_proj: bfloat16 [2, 192, 192], replicated, may hold values from -0.4375 to 0.4375
- w_up: bfloat16 [2, 192, 768], replicated, may hold values from -0.4375 to 0.4375
- w_down: bfloat16 [2, 768, 192], replicated, may hold values from -0.21875 to 0.21875
- tables: float32 [2, 4, 16, 6, 3312], P(None, None, 'lat'), may hold values from -4 to 4
Outputs:
- result: bfloat16 [8, 96, 192, 192], P(None, 'lat', 'lon')
All inputs are finite; a program needn't handle non-finite values.
Results may differ from a plain program's by a relative error of at most 0.02.
Values may be sent and summed in bfloat16 or wider, within the bound.
No kernel may reach another device: no remote copies, remote signals or barrier semaphores. Data moves between devices by JAX's collectives and lax.ppermute only.
A program may use at most 128 MiB of HBM per device.

v0:
```python
import functools
import math

import jax
import jax.numpy as jnp
import ml_dtypes
import numpy as np
from jax import lax
from jax.experimental import pallas as pl
from jax.experimental.pallas import tpu as pltpu
from jax.sharding import PartitionSpec as P

C = 192
HEADS = 6
HEAD = 32
FF = 768
Z = 8
WZ = 2
WLAT = 6
WLON = 12
HLAT = 3
HLON = 6
SPAN = WZ * WLAT * WLON
QB = WZ * HLAT * HLON
QUAD = Z * HLAT * HLON
BAND = 2 * WLON - 1
TROW = WLAT * BAND
TW = 384
TILES = TW // 128
QL = HEADS * QB
PEN = 300

EPS = 1e-05
LOG2E = math.log2(math.e)
BIG = -1e30
F32 = jnp.float32
BF16 = jnp.bfloat16
NT = (((1,), (1,)), ((), ()))


def key_select(masked):
    sel = np.zeros((SPAN, TW), np.float32)
    for part_a in range(2):
        for part_b in range(2):
            for zj in range(WZ):
                for r in range(HLAT):
                    for o in range(HLON):
                        row = (part_a * 2 + part_b) * QB + zj * 18 + r * 6 + o
                        rj = part_a * HLAT + r
                        oj = part_b * HLON + o
                        sel[row, zj * TROW + rj * BAND + oj + WLON - 1] = 1
                        if masked:
                            sel[row, PEN + zj] = 1
                            sel[row, PEN + 2 + part_a] = 1
    return sel.astype(ml_dtypes.bfloat16)


def fold_matrix():
    fold = np.zeros((40, QL), np.float32)
    for lane in range(QL):
        fold[lane % QB, lane] = 1
    return fold.astype(ml_dtypes.bfloat16)


def head_mask():
    rows = np.arange(C)[:, None] // HEAD
    lanes = np.arange(QL)[None, :] // QB
    return (rows == lanes).astype(np.float32)


def normalize(values, gain):
    mean = jnp.mean(values, axis=-1, keepdims=True)
    centered = values - mean
    var = jnp.mean(centered * centered, axis=-1, keepdims=True)
    return (centered * lax.rsqrt(var + EPS) * gain).astype(BF16)


def dot(a, b):
    return jnp.dot(a, b, preferred_element_type=F32)


def dot_nt(a, b):
    return lax.dot_general(a, b, NT, preferred_element_type=F32)


def table_rows(table, base, half, rows_ref):
    blank = jnp.zeros((HEADS, TW - 2 * TROW), F32)
    for zi in range(WZ):
        for r in range(HLAT):
            at = [((zi * WZ + zj) * WLAT + half * HLAT + r) * TROW for zj in range(WZ)]
            wide = jnp.concatenate([table[:, k : k + TROW] for k in at] + [blank], axis=1)
            for t in range(TILES):
                rows_ref[t, pl.ds(base + zi * HLAT + r, HEADS, stride=6), :] = (
                    wide[:, t * 128 : (t + 1) * 128]
                )


def joined(tiles):
    return jnp.concatenate([tiles[t] for t in range(TILES)], axis=-1)


def expand_rows(rows, first, chunk, wide_ref):
    for o in range(HLON):
        shift = first + o
        rolled = pltpu.roll(rows, shift, 1) if shift else rows
        for t in range(TILES):
            wide_ref[chunk, t, pl.ds(o, QB, stride=6), :] = rolled[:QB, t * 128 : (t + 1) * 128]


def attend(keys, values_t, query, wide, select, fold, hmask, stack_ref):
    lanes = lax.broadcasted_iota(jnp.int32, (1, C), 1)
    for h in range(HEADS):
        own = (lanes >= h * HEAD) & (lanes < (h + 1) * HEAD)
        stack_ref[h * QB : (h + 1) * QB, :] = jnp.where(own, query, 0.0)
    scores = dot_nt(keys, stack_ref[...].astype(BF16)) + dot_nt(select, wide)
    top = jnp.max(scores, axis=0, keepdims=True)
    weights = jnp.exp2(scores - top)
    total = jnp.sum(weights, axis=0, keepdims=True)
    mixed = dot(values_t, weights.astype(BF16))
    mixed = (mixed * (hmask * (1.0 / total))).astype(BF16)
    return dot_nt(fold, mixed)[:QB]


def feed_forward(resid, mixed, gain_two, w_proj, w_up, w_down):
    first = (resid + dot(mixed, w_proj)).astype(BF16)
    first32 = first.astype(F32)
    inner = normalize(first32, gain_two)
    hidden = dot(inner, w_up)
    hidden = (hidden * 0.5 * (1.0 + lax.erf(hidden * (0.5**0.5)))).astype(BF16)
    return first32 + dot(hidden, w_down)


QSCALE = HEAD**-0.5 * LOG2E


def first_kernel(
    x_ref, gains_ref, wqkv_ref, wproj_ref, wup_ref, wdown_ref, tab_ref, tab1_ref,
    select_ref, fold_ref, hmask_ref,
    left_ref, right_ref, tabhi_ref,
    tok_ref, q_ref, o_ref, rows_ref, hi_ref, wide_ref, stack_ref, quad_ref,
):
    for z in range(Z):
        for r in range(WLAT):
            row = x_ref[z, r].astype(F32)
            base = (z // 2) * SPAN + (r // HLAT) * 2 * QB + (z % 2) * 18 + (r % HLAT) * 6
            tok_ref[base : base + 6, :] = row[:6]
            tok_ref[base + QB : base + QB + 6, :] = row[6:]
    hi_ref[...] = jnp.zeros_like(hi_ref)
    rows_ref[...] = jnp.zeros_like(rows_ref)
    for w in range(4):
        table_rows(tab1_ref[0, w, 0] * LOG2E, w * QB, 1, hi_ref)
    hi = joined(hi_ref).astype(BF16)
    tabhi_ref[0] = hi[:, :C]
    tabhi_ref[1] = hi[:, C:]
    gain_one = gains_ref[0, 0:1]
    gain_two = gains_ref[0, 1:2]
    wqk = wqkv_ref[0, :, : 2 * C]
    wv_t = wqkv_ref[0, :, 2 * C :].T
    select = select_ref[...]
    fold = fold_ref[...]
    hmask = hmask_ref[...]
    for w in range(4):
        table = tab_ref[0, w, 0] * LOG2E
        normed = normalize(tok_ref[w * SPAN : (w + 1) * SPAN, :], gain_one)
        both = dot(normed, wqk)
        q_ref[...] = both[:, :C] * QSCALE
        keys = both[:, C:].astype(BF16)
        values_t = dot_nt(wv_t, normed).astype(BF16)
        for a in range(2):
            table_rows(table, 0, a, rows_ref)
            rows = joined(rows_ref)
            for b in range(2):
                block = a * 2 + b
                chunk = w * 4 + block
                expand_rows(rows, b * HLON, block, wide_ref)
                o_ref[chunk * QB : (chunk + 1) * QB, :] = attend(
                    keys, values_t, q_ref[block * QB : (block + 1) * QB, :],
                    joined(wide_ref.at[block]).astype(BF16), select, fold, hmask, stack_ref,
                )
    tok_ref[...] = feed_forward(
        tok_ref[...], o_ref[...].astype(BF16), gain_two, wproj_ref[0], wup_ref[0], wdown_ref[0]
    )
    for b, out_ref in ((0, left_ref), (1, right_ref)):
        for a in range(2):
            for z in range(Z):
                base = (z // 2) * SPAN + (a * 2 + b) * QB + (z % 2) * 18
                to = (z + Z - 1) % Z * 18
                quad_ref[to : to + 18, :] = tok_ref[base : base + 18, :]
            out_ref[a] = quad_ref[...].astype(BF16)


def second_kernel(
    flags_ref, left_ref, right_ref, fl_ref, fr_ref, prev_ref, next_ref,
    gains_ref, wqkv_ref, wproj_ref, wup_ref, wdown_ref, tab_ref,
    select_ref, fold_ref, hmask_ref,
    out_ref,
    own_ref, xw_ref, q_ref, o_ref, rows_ref, wide_ref, stack_ref, quad_ref, nat_ref,
):
    gain_one = gains_ref[1, 0:1]
    gain_two = gains_ref[1, 1:2]
    wq = wqkv_ref[0, :, :C]
    wk = wqkv_ref[0, :, C : 2 * C]
    wv_t = wqkv_ref[0, :, 2 * C :].T
    select = select_ref[...]
    fold = fold_ref[...]
    hmask = hmask_ref[...]
    for b, ref in ((0, left_ref), (1, right_ref)):
        for a in range(2):
            at = (b * 2 + a) * QUAD
            own_ref[at : at + QUAD, :] = ref[a].astype(F32)
    q_ref[...] = dot(normalize(own_ref[...], gain_one), wq) * QSCALE
    lane = lax.broadcasted_iota(jnp.int32, (QL, 128), 1) + 256
    zi = (lax.broadcasted_iota(jnp.int32, (QL, 1), 0) % QB) // 18
    pen_z = jnp.where(((lane == PEN) & (zi == 1)) | ((lane == PEN + 1) & (zi == 0)), BIG, 0.0)
    first_rows = flags_ref[0]
    last_rows = flags_ref[1]
    lane_row = lane[:1]
    pen_prev = jnp.where((lane_row == PEN + 2) & (first_rows == 1), BIG, 0.0)
    pen_own = jnp.where((lane_row == PEN + 3) & (last_rows == 1), BIG, 0.0)
    rows_ref[...] = jnp.zeros_like(rows_ref)
    quad_ref[...] = prev_ref[4].astype(F32)
    nat_ref[:QUAD, :] = prev_ref[5].astype(F32)
    for zw in range(4):
        for a in range(2):
            if a == 0:
                part = slice(zw * QB, (zw + 1) * QB)
                rows = jnp.concatenate([quad_ref[part, :], nat_ref[part, :]], axis=1)
            else:
                table_rows(tab_ref[0, zw, 0] * LOG2E, 0, 0, rows_ref)
                rows = joined(rows_ref)[:QB]
            for b in range(2):
                chunk = (b * 2 + a) * 4 + zw
                expand_rows(rows, (1 - b) * HLON, chunk, wide_ref)
                tail = wide_ref[chunk, 2] + (pen_prev if a == 0 else pen_own)
                if zw == 3:
                    tail = tail + pen_z
                wide_ref[chunk, 2] = tail
    for a in range(2):
        for part_a in range(2):
            away = part_a == a
            if not away:
                cols = [fl_ref.at[a], left_ref.at[a], right_ref.at[a], fr_ref.at[a]]
            else:
                src = prev_ref if a == 0 else next_ref
                cols = [src.at[2], src.at[0], src.at[1], src.at[3]]
            for b in range(2):
                for part_b in range(2):
                    quad_ref[...] = cols[b * 2 + part_b][...].astype(F32)
                    at = (part_a * 2 + part_b) * QB
                    for zw in range(4):
                        chunk = (b * 2 + a) * 4 + zw
                        xw_ref[chunk, at : at + QB, :] = quad_ref[zw * QB : (zw + 1) * QB, :]
    for chunk in range(16):
        normed = normalize(xw_ref[chunk], gain_one)
        keys = dot(normed, wk).astype(BF16)
        values_t = dot_nt(wv_t, normed).astype(BF16)
        o_ref[chunk * QB : (chunk + 1) * QB, :] = attend(
            keys, values_t, q_ref[chunk * QB : (chunk + 1) * QB, :],
            joined(wide_ref.at[chunk]).astype(BF16), select, fold, hmask, stack_ref,
        )
    own_ref[...] = feed_forward(
        own_ref[...], o_ref[...].astype(BF16), gain_two, wproj_ref[0], wup_ref[0], wdown_ref[0]
    )
    for b in range(2):
        for z in range(Z):
            for r in range(WLAT):
                rolled = (z + Z - 1) % Z
                base = (b * 2 + r // HLAT) * QUAD + rolled * 18 + (r % HLAT) * 6
                at = (z * WLAT + r) * 16 + b * HLON
                nat_ref[at : at + HLON, :] = own_ref[base : base + HLON, :]
    for z in range(Z):
        for r in range(WLAT):
            at = (z * WLAT + r) * 16
            out_ref[z, r] = nat_ref[at : at + WLON, :].astype(BF16)


def whole(shape):
    return pl.BlockSpec(shape, lambda *_: (0,) * len(shape))


def picked(shape, layer):
    return pl.BlockSpec((1,) + shape[1:], lambda *_: (layer,) + (0,) * (len(shape) - 1))


def weight_specs(layer, gains, w_qkv, w_proj, w_up, w_down):
    return [whole(gains.shape)] + [picked(w.shape, layer) for w in (w_qkv, w_proj, w_up, w_down)]


PARAMS = pltpu.CompilerParams(vmem_limit_bytes=56 * 1024 * 1024)


def shifted(value, axis, steps):
    count = lax.axis_size(axis)
    pairs = [(source, (source + steps) % count) for source in range(count)]
    return lax.ppermute(value, axis, pairs)


def shards(grid, gains, w_qkv, w_proj, w_up, w_down, tables):
    plain = jnp.asarray(key_select(False))
    masked = jnp.asarray(key_select(True))
    fold = jnp.asarray(fold_matrix())
    hmask = jnp.asarray(head_mask())
    weights = (gains, w_qkv, w_proj, w_up, w_down)
    half = jax.ShapeDtypeStruct((2, QUAD, C), BF16)
    left, right, tabhi = pl.pallas_call(
        first_kernel,
        grid=(1,),
        in_specs=[whole(grid.shape)]
        + weight_specs(0, *weights)
        + [picked(tables.shape, 0), picked(tables.shape, 1)]
        + [whole(plain.shape), whole(fold.shape), whole(hmask.shape)],
        out_specs=[whole(half.shape)] * 3,
        out_shape=[half, half, half],
        scratch_shapes=[
            pltpu.VMEM((4 * SPAN, C), F32),
            pltpu.VMEM((SPAN, C), F32),
            pltpu.VMEM((4 * SPAN, C), F32),
            pltpu.VMEM((TILES, 40, 128), F32),
            pltpu.VMEM((TILES, 4 * QB, 128), F32),
            pltpu.VMEM((4, TILES, QL, 128), F32),
            pltpu.VMEM((QL, C), F32),
            pltpu.VMEM((QUAD, C), F32),
        ],
        compiler_params=PARAMS,
        name="first_layer",
    )(grid, *weights, tables, tables, plain, fold, hmask)
    from_left = shifted(right, "lon", 1)
    from_right = shifted(left, "lon", -1)
    down = jnp.concatenate([left[1:], right[1:], from_left[1:], from_right[1:], tabhi])
    up = jnp.concatenate([left[:1], right[:1], from_left[:1], from_right[:1]])
    from_prev = shifted(down, "lat", 1)
    from_next = shifted(up, "lat", -1)
    lat = lax.axis_index("lat")
    flags = jnp.stack([lat == 0, lat == lax.axis_size("lat") - 1]).astype(jnp.int32)
    moved = (left, right, from_left, from_right, from_prev, from_next)
    return pl.pallas_call(
        second_kernel,
        grid=(1,),
        in_specs=[pl.BlockSpec(memory_space=pltpu.SMEM)]
        + [whole(m.shape) for m in moved]
        + weight_specs(1, *weights)
        + [picked(tables.shape, 1)]
        + [whole(masked.shape), whole(fold.shape), whole(hmask.shape)],
        out_specs=whole(grid.shape),
        out_shape=jax.ShapeDtypeStruct(grid.shape, BF16),
        scratch_shapes=[
            pltpu.VMEM((4 * QUAD, C), F32),
            pltpu.VMEM((16, SPAN, C), F32),
            pltpu.VMEM((4 * QUAD, C), F32),
            pltpu.VMEM((4 * QUAD, C), F32),
            pltpu.VMEM((TILES, 40, 128), F32),
            pltpu.VMEM((16, TILES, QL, 128), F32),
            pltpu.VMEM((QL, C), F32),
            pltpu.VMEM((QUAD, C), F32),
            pltpu.VMEM((Z * WLAT * 16, C), F32),
        ],
        compiler_params=PARAMS,
        name="second_layer",
    )(flags, *moved, *weights, tables, masked, fold, hmask)


def solution(mesh):
    in_specs = (
        P(None, "lat", "lon", None),
        P(),
        P(),
        P(),
        P(),
        P(),
        P(None, None, "lat", None, None),
    )
    out_specs = P(None, "lat", "lon", None)
    return jax.shard_map(shards, mesh=mesh, in_specs=in_specs, out_specs=out_specs, check_vma=False)
```

profile of v0, /device:TPU:1, one launch (start us, length us, event | category | flops | bytes accessed | tf_op | source)
XLA Modules:
  0.0 62.5 jit_solution(14581645444809569615)
XLA Ops:
  0.0 0.0 copy-start.3
  0.0 2.2 %copy.14.tab_ref.tab1_ref = f32[2,4,1,6,3312]{4,3,2,1,0:T(8,128)} copy(f32[2,4,1,6,3312]{4,2,3,1,0:T(1,128)} %param.17) | data formatting | bytes 1271808 | tf_op args[6]
  2.2 0.0 copy-done.3
  2.2 0.0 copy-start.6
  2.2 1.2 %copy.13.wdown_ref = bf16[2,768,192]{2,1,0:T(8,128)(2,1)} copy(bf16[2,768,192]{1,2,0:T(8,128)(2,1)S(1)} %copy-done.3) | data formatting | bytes 1179648 | tf_op args[5]
  3.4 0.0 copy-done.6
  3.4 0.8 %copy.12.x_ref = bf16[8,6,12,192]{3,2,1,0:T(8,128)(2,1)} copy(bf16[8,6,12,192]{3,0,2,1:T(8,128)(2,1)S(1)} %copy-done.6) | data formatting | bytes 442368 | tf_op args[0]
  4.2 13.1 %first_layer.1 = (bf16[2,144,192]{2,1,0:T(8,128)(2,1)}, bf16[2,144,192]{2,1,0:T(8,128)(2,1)}, bf16[2,144,192]{2,1,0:T(8,128)(2,1)}) custom-call(bf16[8,6,12,192]{3,2,1,0:T(8,128)(2,1)} %copy.12.x_ref, f32[2,2,192]{2,1,0:T(2,128)} %gains_ref.3, bf16[2,192,576]{2,1,0:T(8,128)(2,1)} %wqkv_ref.3, bf16[2,192,192]{2,1,0:T(8,128)(2,1)} %wproj_ref.3, ...), custom_call_target="tpu_custom_call" | custom-call | tf_op jit(solution)/shard_map/first_layer/pallas_call | solution.py:305
  17.3 3.7 %collective-permute-start = (bf16[2,144,192]{2,1,0:T(8,128)(2,1)}, bf16[2,144,192]{2,1,0:T(8,128)(2,1)S(1)}, u32[]{:S(2)}, u32[]{:S(2)}) collective-permute-start(bf16[2,144,192]{2,1,0:T(8,128)(2,1)} %get-tuple-element.9.right_ref), channel_id=1, source_target_pairs={{0,16},{16,32},{32,48},{48,64},{64,80},{80,96},{96,112},{112,128},... | collective-permute-start | bytes 331784 | tf_op jit(solution)/shard_map/ppermute | solution.py:295
  21.0 0.0 copy-start
  21.0 5.4 %collective-permute-start.1 = (bf16[2,144,192]{2,1,0:T(8,128)(2,1)}, bf16[2,144,192]{2,1,0:T(8,128)(2,1)S(1)}, u32[]{:S(2)}, u32[]{:S(2)}) collective-permute-start(bf16[2,144,192]{2,1,0:T(8,128)(2,1)} %get-tuple-element.8.left_ref), channel_id=1, source_target_pairs={{0,240},{16,0},{32,16},{48,32},{64,48},{80,64},{96,80},{112,96},{1... | collective-permute-start | bytes 331784 | tf_op jit(solution)/shard_map/ppermute | solution.py:295
  26.4 1.0 %fusion = (bf16[1,144,192]{2,1,0:T(8,128)(2,1)S(1)}, bf16[6,144,192]{2,1,0:T(8,128)(2,1)S(1)}) fusion(bf16[2,144,192]{2,1,0:T(8,128)(2,1)} %get-tuple-element.8.left_ref), kind=kLoop, calls=%fused_computation.7 | loop fusion | bytes 258048 | tf_op jit(solution)/shard_map/slice | solution.py:330
  27.4 0.0 copy-done
  27.4 2.7 %collective-permute-done.fl_ref = bf16[2,144,192]{2,1,0:T(8,128)(2,1)S(1)} collective-permute-done((bf16[2,144,192]{2,1,0:T(8,128)(2,1)}, bf16[2,144,192]{2,1,0:T(8,128)(2,1)S(1)}, u32[]{:S(2)}, u32[]{:S(2)}) %collective-permute-start) | collective-permute-done | bytes 110624 | tf_op jit(solution)/shard_map/ppermute | solution.py:295
  30.2 0.0 copy-start.1
  30.2 0.6 %copy-done.1 = bf16[2,144,192]{2,1,0:T(8,128)(2,1)} copy-done((bf16[2,144,192]{2,1,0:T(8,128)(2,1)}, bf16[2,144,192]{2,1,0:T(8,128)(2,1)S(1)}, u32[]{:S(2)}) %copy-start.1) | copy-done | bytes 110616
  30.8 0.0 collective-permute-done.1.fr_ref
  30.8 0.0 copy-start.2
  30.8 0.0 copy-start.7
  30.8 0.6 %copy-done.2 = bf16[2,144,192]{2,1,0:T(8,128)(2,1)} copy-done((bf16[2,144,192]{2,1,0:T(8,128)(2,1)}, bf16[2,144,192]{2,1,0:T(8,128)(2,1)S(1)}, u32[]{:S(2)}) %copy-start.2) | copy-done | bytes 110616
  31.5 0.3 copy-done.7
  31.8 1.7 %collective-permute-start.2 = (bf16[6,144,192]{2,1,0:T(8,128)(2,1)S(1)}, bf16[6,144,192]{2,1,0:T(8,128)(2,1)S(1)}, u32[]{:S(2)}, u32[]{:S(2)}) collective-permute-start(bf16[6,144,192]{2,1,0:T(8,128)(2,1)S(1)} %constant_dynamic-update-slice_fusion), channel_id=1, source_target_pairs={{0,1},{1,2},{2,3},{3,4},{4,5},{5,6},{6,7},{7,8},{8,9},{9,10},{10,1... | collective-permute-start | bytes 995336 | tf_op jit(solution)/shard_map/ppermute | solution.py:295
  33.5 0.1 pad_maximum_fusion
  33.6 0.3 collective-permute-start.3
  33.9 0.7 %add_convert_fusion.flags_ref = s32[2]{0:T(128)} fusion(pred[1]{0:T(512)(128)(4,1)} %bitcast.1, pred[1]{0:T(512)(128)(4,1)} %bitcast), kind=kLoop, calls=%fused_computation.6 | loop fusion | flops 4 | bytes 10 | tf_op jit(solution)/shard_map/convert_element_type | solution.py:334
  34.5 10.2 %collective-permute-done.3.next_ref = bf16[4,144,192]{2,1,0:T(8,128)(2,1)S(1)} collective-permute-done((bf16[4,144,192]{2,1,0:T(8,128)(2,1)S(1)}, bf16[4,144,192]{2,1,0:T(8,128)(2,1)S(1)}, u32[]{:S(2)}, u32[]{:S(2)}) %collective-permute-start.3) | collective-permute-done | bytes 221216 | tf_op jit(solution)/shard_map/ppermute | solution.py:295
  44.7 0.0 copy-start.5
  44.7 0.0 collective-permute-done.2.prev_ref
  44.7 0.7 %copy-done.5 = bf16[4,144,192]{2,1,0:T(8,128)(2,1)} copy-done((bf16[4,144,192]{2,1,0:T(8,128)(2,1)}, bf16[4,144,192]{2,1,0:T(8,128)(2,1)S(1)}, u32[]{:S(2)}) %copy-start.5) | copy-done | bytes 221208
  45.5 0.8 %copy-done.4 = bf16[6,144,192]{2,1,0:T(8,128)(2,1)} copy-done((bf16[6,144,192]{2,1,0:T(8,128)(2,1)}, bf16[6,144,192]{2,1,0:T(8,128)(2,1)S(1)}, u32[]{:S(2)}) %copy-start.4) | copy-done | bytes 331800
  46.2 14.4 %second_layer.1 = bf16[8,6,12,192]{3,2,1,0:T(8,128)(2,1)} custom-call(s32[2]{0:T(128)} %add_convert_fusion.flags_ref, bf16[2,144,192]{2,1,0:T(8,128)(2,1)} %get-tuple-element.8.left_ref, bf16[2,144,192]{2,1,0:T(8,128)(2,1)} %get-tuple-element.9.right_ref, bf16[2,144,192]{2,1,0:T(8,128)(2,1)} %copy-done.1, bf16[2,144,192]{2,1,0:T(8,128)(2,1)} %copy-done.2, ...), custom_call_target="tpu_custom_call" | custom-call | tf_op jit(solution)/shard_map/second_layer/pallas_call | solution.py:336
  60.6 1.9 %copy.18 = bf16[8,6,12,192]{3,0,2,1:T(8,128)(2,1)} copy(bf16[8,6,12,192]{3,2,1,0:T(8,128)(2,1)} %second_layer.1) | data formatting | bytes 442368 | tf_op jit(solution)/shard_map/second_layer/pallas_call | solution.py:336
  (5 shorter events, 0.0 us)
Async XLA Ops:
  0.0 2.2 %copy-start.3 = (bf16[2,768,192]{1,2,0:T(8,128)(2,1)S(1)}, bf16[2,768,192]{1,2,0:T(8,128)(2,1)}, u32[]{:S(2)}) copy-start(bf16[2,768,192]{1,2,0:T(8,128)(2,1)} %param.16) | copy-start | bytes 1769476
  2.2 1.2 %copy-start.6 = (bf16[8,6,12,192]{3,0,2,1:T(8,128)(2,1)S(1)}, bf16[8,6,12,192]{3,0,2,1:T(8,128)(2,1)}, u32[]{:S(2)}) copy-start(bf16[8,6,12,192]{3,0,2,1:T(8,128)(2,1)} %param.11) | copy-start | bytes 663556
  17.3 12.9 %collective-permute-start = (bf16[2,144,192]{2,1,0:T(8,128)(2,1)}, bf16[2,144,192]{2,1,0:T(8,128)(2,1)S(1)}, u32[]{:S(2)}, u32[]{:S(2)}) collective-permute-start(bf16[2,144,192]{2,1,0:T(8,128)(2,1)} %get-tuple-element.9.right_ref), channel_id=1, source_target_pairs={{0,16},{16,32},{32,48},{48,64},{64,80},{80,96},{96,112},{112,128},... | collective-permute-start | bytes 331784 | tf_op jit(solution)/shard_map/ppermute | solution.py:295
  21.0 6.4 %copy-start = (bf16[2,144,192]{2,1,0:T(8,128)(2,1)S(1)}, bf16[2,144,192]{2,1,0:T(8,128)(2,1)}, u32[]{:S(2)}) copy-start(bf16[2,144,192]{2,1,0:T(8,128)(2,1)} %get-tuple-element.9.right_ref) | copy-start | bytes 331780
  21.0 9.8 %collective-permute-start.1 = (bf16[2,144,192]{2,1,0:T(8,128)(2,1)}, bf16[2,144,192]{2,1,0:T(8,128)(2,1)S(1)}, u32[]{:S(2)}, u32[]{:S(2)}) collective-permute-start(bf16[2,144,192]{2,1,0:T(8,128)(2,1)} %get-tuple-element.8.left_ref), channel_id=1, source_target_pairs={{0,240},{16,0},{32,16},{48,32},{64,48},{80,64},{96,80},{112,96},{1... | collective-permute-start | bytes 331784 | tf_op jit(solution)/shard_map/ppermute | solution.py:295
  30.2 0.7 %copy-start.1 = (bf16[2,144,192]{2,1,0:T(8,128)(2,1)}, bf16[2,144,192]{2,1,0:T(8,128)(2,1)S(1)}, u32[]{:S(2)}) copy-start(bf16[2,144,192]{2,1,0:T(8,128)(2,1)S(1)} %collective-permute-done.fl_ref) | copy-start | bytes 331780
  30.8 0.7 %copy-start.2 = (bf16[2,144,192]{2,1,0:T(8,128)(2,1)}, bf16[2,144,192]{2,1,0:T(8,128)(2,1)S(1)}, u32[]{:S(2)}) copy-start(bf16[2,144,192]{2,1,0:T(8,128)(2,1)S(1)} %collective-permute-done.1.fr_ref) | copy-start | bytes 331780
  30.8 1.0 %copy-start.7 = (bf16[2,144,192]{2,1,0:T(8,128)(2,1)S(1)}, bf16[2,144,192]{2,1,0:T(8,128)(2,1)}, u32[]{:S(2)}) copy-start(bf16[2,144,192]{2,1,0:T(8,128)(2,1)} %get-tuple-element.10) | copy-start | bytes 331780
  31.8 12.9 %collective-permute-start.2 = (bf16[6,144,192]{2,1,0:T(8,128)(2,1)S(1)}, bf16[6,144,192]{2,1,0:T(8,128)(2,1)S(1)}, u32[]{:S(2)}, u32[]{:S(2)}) collective-permute-start(bf16[6,144,192]{2,1,0:T(8,128)(2,1)S(1)} %constant_dynamic-update-slice_fusion), channel_id=1, source_target_pairs={{0,1},{1,2},{2,3},{3,4},{4,5},{5,6},{6,7},{7,8},{8,9},{9,10},{10,1... | collective-permute-start | bytes 995336 | tf_op jit(solution)/shard_map/ppermute | solution.py:295
  33.6 11.1 %collective-permute-start.3 = (bf16[4,144,192]{2,1,0:T(8,128)(2,1)S(1)}, bf16[4,144,192]{2,1,0:T(8,128)(2,1)S(1)}, u32[]{:S(2)}, u32[]{:S(2)}) collective-permute-start(bf16[4,144,192]{2,1,0:T(8,128)(2,1)S(1)} %pad_maximum_fusion), channel_id=1, source_target_pairs={{0,15},{1,0},{2,1},{3,2},{4,3},{5,4},{6,5},{7,6},{8,7},{9,8},{10,9... | collective-permute-start | bytes 663560 | tf_op jit(solution)/shard_map/ppermute | solution.py:295
  44.7 0.7 %copy-start.5 = (bf16[4,144,192]{2,1,0:T(8,128)(2,1)}, bf16[4,144,192]{2,1,0:T(8,128)(2,1)S(1)}, u32[]{:S(2)}) copy-start(bf16[4,144,192]{2,1,0:T(8,128)(2,1)S(1)} %collective-permute-done.3.next_ref) | copy-start | bytes 663556
  45.5 0.8 %copy-start.4 = (bf16[6,144,192]{2,1,0:T(8,128)(2,1)}, bf16[6,144,192]{2,1,0:T(8,128)(2,1)S(1)}, u32[]{:S(2)}) copy-start(bf16[6,144,192]{2,1,0:T(8,128)(2,1)S(1)} %collective-permute-done.2.prev_ref) | copy-start | bytes 995332
where the time goes:
time: 62.8 us; the launch traced here: 62.5 us
  Pallas kernels  27.5 us (44%)
  waiting for transfers between devices  13 us (21%)
  starting transfers between devices  11.1 us (18%)
  local copies, waits for them, and re-layouts  10.2 us (16%)
  other arithmetic  0.73 us (1%)
    pallas_call x1, Pallas kernels, shards(): pl.pallas_call(second_kernel, grid=(1,), in_specs=[pl.BlockSpec(memory_sp...  14.4 us
    pallas_call x1, Pallas kernels, shards(): pl.pallas_call(first_kernel, grid=(1,), in_specs=[whole(grid.shape)] + we...  13.1 us
    ppermute x4, waiting for transfers between devices, shifted(): return lax.ppermute(value, axis, pairs)  13 us
    ppermute x4, starting transfers between devices, shifted(): return lax.ppermute(value, axis, pairs)  11.1 us
    unnamed x19, local copies, waits for them, and re-layouts  7.29 us
    pallas_call x1, local copies, waits for them, and re-layouts, shards(): pl.pallas_call(second_kernel, grid=(1,), in_specs=[pl.BlockSpec(memory_sp...  1.87 us
  transfers between devices with their start and end apart: 4, of which 2 were waited for; matrix products, arithmetic and copies ran while one was open for 3% of the time, Pallas kernels for 0%

commit v1 on v0

v1 whole, which is shorter than its diff:
```python
import functools
import math

import jax
import jax.numpy as jnp
import ml_dtypes
import numpy as np
from jax import lax
from jax.experimental import pallas as pl
from jax.experimental.pallas import tpu as pltpu
from jax.sharding import PartitionSpec as P

C = 192
HEADS = 6
HEAD = 32
FF = 768
Z = 8
WZ = 2
WLAT = 6
WLON = 12
HLAT = 3
HLON = 6
SPAN = WZ * WLAT * WLON
QB = WZ * HLAT * HLON
QUAD = Z * HLAT * HLON
BAND = 2 * WLON - 1
TROW = WLAT * BAND
TW = 384
TILES = TW // 128
QP = 40
SP = 4 * QP
QL = HEADS * QP
PEN = 300
ONE = 330
TSPAN = 168

EPS = 1e-05
LOG2E = math.log2(math.e)
BIG = -1e30
F32 = jnp.float32
BF16 = jnp.bfloat16
NT = (((1,), (1,)), ((), ()))


def key_select(masked):
    sel = np.zeros((TW, SP), np.float32)
    for part in range(4):
        for zj in range(WZ):
            for r in range(HLAT):
                for o in range(HLON):
                    col = part * QP + zj * 18 + r * 6 + o
                    rj = part // 2 * HLAT + r
                    oj = part % 2 * HLON + o
                    sel[zj * TROW + rj * BAND + oj + WLON - 1, col] = 1
                    if masked:
                        sel[PEN + zj, col] = 1
                        sel[PEN + 2 + part // 2, col] = 1
        sel[ONE : ONE + WLON, part * QP + QB : (part + 1) * QP] = BIG
    return sel.astype(ml_dtypes.bfloat16)


def normalize(values, gain):
    mean = jnp.mean(values, axis=-1, keepdims=True)
    centered = values - mean
    var = jnp.mean(centered * centered, axis=-1, keepdims=True)
    return (centered * lax.rsqrt(var + EPS) * gain).astype(BF16)


def dot(a, b):
    return jnp.dot(a, b, preferred_element_type=F32)


def dot_nt(a, b):
    return lax.dot_general(a, b, NT, preferred_element_type=F32)


def table_rows(table, base, half, stride, rows_ref):
    blank = jnp.zeros((HEADS, TW - 2 * TROW), F32)
    lane = lax.broadcasted_iota(jnp.int32, blank.shape, 1) + 2 * TROW
    blank = jnp.where(lane == ONE, 1.0, blank)
    for zi in range(WZ):
        for r in range(HLAT):
            at = [((zi * WZ + zj) * WLAT + half * HLAT + r) * TROW for zj in range(WZ)]
            wide = jnp.concatenate([table[:, k : k + TROW] for k in at] + [blank], axis=1)
            for t in range(TILES):
                rows_ref[t, pl.ds(base + zi * HLAT + r, HEADS, stride=stride), :] = (
                    wide[:, t * 128 : (t + 1) * 128]
                )


def joined(tiles):
    return jnp.concatenate([tiles[t] for t in range(TILES)], axis=-1)


def expand_rows(rows, first, chunk, wide_ref):
    for o in range(HLON):
        shift = first + o
        rolled = pltpu.roll(rows, shift, 1) if shift else rows
        for h in range(HEADS):
            for t in range(TILES):
                wide_ref[chunk, t, pl.ds(h * QP + o, 6, stride=6), :] = (
                    rolled[h * 8 : h * 8 + 6, t * 128 : (t + 1) * 128]
                )


def attend(items, select):
    lanes = lax.broadcasted_iota(jnp.int32, (1, C), 1)
    own = [(lanes >= h * HEAD) & (lanes < (h + 1) * HEAD) for h in range(HEADS)]
    stacks = [
        jnp.concatenate([jnp.where(own[h], q, 0.0) for h in range(HEADS)], axis=0).astype(BF16)
        for _, _, q, _ in items
    ]
    scores = [dot_nt(st, it[0]) + dot(it[3], select) for st, it in zip(stacks, items)]
    weights = [
        jnp.exp2(s - jnp.max(s, axis=1, keepdims=True)).astype(BF16) for s in scores
    ]
    mixed = [dot(p, it[1]) for p, it in zip(weights, items)]
    outs = []
    for m in mixed:
        scaled = m[:, :C] * (1.0 / m[:, C : C + 1])
        out = jnp.where(own[0], scaled[:QP], 0.0)
        for h in range(1, HEADS):
            out = jnp.where(own[h], scaled[h * QP : (h + 1) * QP], out)
        outs.append(out)
    return outs


def feed_forward(resid, mixed, gain_two, w_proj, w_up, w_down_t):
    first = (resid + dot(mixed, w_proj)).astype(BF16)
    first32 = first.astype(F32)
    inner = normalize(first32, gain_two)
    hidden = dot(inner, w_up)
    hidden = (hidden * 0.5 * (1.0 + lax.erf(hidden * (0.5**0.5)))).astype(BF16)
    return first32 + dot_nt(hidden, w_down_t)


QSCALE = HEAD**-0.5 * LOG2E


def with_ones(values):
    lanes = lax.broadcasted_iota(jnp.int32, values.shape, 1)
    return jnp.where(lanes == C, 1.0, values).astype(BF16)


def value_weights(wqkv_ref):
    return jnp.concatenate([wqkv_ref[0, :, 2 * C :], jnp.zeros((C, 256 - C), BF16)], axis=1)


def tiles_of(value):
    return value[:, :128], jnp.concatenate([value[:, 128:], value[:, 128:]], axis=1)


def whole_row(first, second):
    return jnp.concatenate([first, second[:, : C - 128]], axis=1)


def first_kernel(
    x_ref, gains_ref, wqkv_ref, wproj_ref, wup_ref, wdown_ref, tab_ref, tab1_ref,
    select_ref,
    left_ref, right_ref, tabhi_ref,
    plain_ref, tok_ref, o_ref, rows_ref, hi_ref, wide_ref,
):
    plain_ref[...] = jnp.zeros_like(plain_ref)
    for r in range(WLAT):
        for o in range(WLON):
            part = r // HLAT * 2 + o // HLON
            at = (r % HLAT) * 6 + o % HLON
            for t, tile in enumerate(tiles_of(x_ref[r, o].astype(F32))):
                plain_ref[part, t, pl.ds(at, Z, stride=18), :] = tile
    for part in range(4):
        for w in range(4):
            rows = pl.ds(w * QB, QP)
            at = (part * 4 + w) * QP
            tok_ref[at : at + QP, :] = whole_row(plain_ref[part, 0, rows, :], plain_ref[part, 1, rows, :])
    for w in range(4):
        table_rows(tab1_ref[0, w, 0] * LOG2E, w * QP, 1, 6, hi_ref)
    hi = joined(hi_ref).astype(BF16)
    for w in range(4):
        tabhi_ref[0, w] = joined(hi_ref.at[:, pl.ds(w * QP, QP)])[:, :C].astype(BF16)
        tabhi_ref[1, w] = joined(hi_ref.at[:, pl.ds(w * QP, QP)])[:, C:].astype(BF16)
    gain_one = gains_ref[0, 0:1]
    gain_two = gains_ref[0, 1:2]
    wqk = wqkv_ref[0, :, : 2 * C]
    wv = value_weights(wqkv_ref)
    select = select_ref[...]
    for w in range(4):
        table = tab_ref[0, w, 0] * LOG2E
        for a in range(2):
            table_rows(table, 0, a, 8, rows_ref.at[a])
            rows = joined(rows_ref.at[a])
            for b in range(2):
                expand_rows(rows, b * HLON, w * 4 + a * 2 + b, wide_ref)
    for w in range(4):
        tokens = jnp.concatenate(
            [tok_ref[(part * 4 + w) * QP : (part * 4 + w + 1) * QP, :] for part in range(4)], axis=0
        )
        normed = normalize(tokens, gain_one)
        both = dot(normed, wqk)
        query = both[:, :C] * QSCALE
        keys = both[:, C:].astype(BF16)
        values = with_ones(dot(normed, wv))
        items = [
            (keys, values, query[part * QP : (part + 1) * QP], joined(wide_ref.at[w * 4 + part]).astype(BF16))
            for part in range(4)
        ]
        for part, out in enumerate(attend(items, select)):
            o_ref[(part * 4 + w) * QP : (part * 4 + w + 1) * QP, :] = out
    tok_ref[...] = feed_forward(
        tok_ref[...], o_ref[...].astype(BF16), gain_two, wproj_ref[0], wup_ref[0], wdown_ref[0]
    )
    for b, out_ref in ((0, left_ref), (1, right_ref)):
        for a in range(2):
            part = a * 2 + b
            for w in range(4):
                at = (part * 4 + w) * QP
                for t, tile in enumerate(tiles_of(tok_ref[at : at + QB, :])):
                    plain_ref[part, t, pl.ds(w * QB, QB), :] = tile
                    if w == 0:
                        plain_ref[part, t, pl.ds(QUAD, 18), :] = tile[:18]
            for zw in range(4):
                rows = pl.ds(zw * QB + 18, QP)
                out_ref[a, zw] = whole_row(plain_ref[part, 0, rows, :], plain_ref[part, 1, rows, :]).astype(BF16)


def second_kernel(
    flags_ref, left_ref, right_ref, fl_ref, fr_ref, prev_ref, next_ref,
    gains_ref, wqkv_ref, wproj_ref, wup_ref, wdown_ref, tab_ref,
    select_ref,
    out_ref,
    plain_ref, own_ref, q_ref, o_ref, rows_ref, hi_ref, wide_ref,
):
    gain_one = gains_ref[1, 0:1]
    gain_two = gains_ref[1, 1:2]
    wq = wqkv_ref[0, :, :C]
    wk = wqkv_ref[0, :, C : 2 * C]
    wv = value_weights(wqkv_ref)
    select = select_ref[...]
    for b, ref in ((0, left_ref), (1, right_ref)):
        for a in range(2):
            for zw in range(4):
                at = ((b * 2 + a) * 4 + zw) * QP
                own_ref[at : at + QP, :] = ref[a, zw].astype(F32)
    q_ref[...] = dot(normalize(own_ref[...], gain_one), wq) * QSCALE
    lane = lax.broadcasted_iota(jnp.int32, (QL, 128), 1) + 256
    zi = (lax.broadcasted_iota(jnp.int32, (QL, 1), 0) % QP) // 18
    pen_z = jnp.where(((lane == PEN) & (zi == 1)) | ((lane == PEN + 1) & (zi == 0)), BIG, 0.0)
    lane_row = lane[:1]
    pen_prev = jnp.where((lane_row == PEN + 2) & (flags_ref[0] == 1), BIG, 0.0)
    pen_own = jnp.where((lane_row == PEN + 3) & (flags_ref[1] == 1), BIG, 0.0)
    for zw in range(4):
        table_rows(tab_ref[0, zw, 0] * LOG2E, 0, 0, 8, rows_ref.at[1])
        hi = jnp.concatenate([prev_ref[4, zw], prev_ref[5, zw]], axis=1).astype(F32)
        for t in range(TILES):
            hi_ref[t] = hi[:, t * 128 : (t + 1) * 128]
            for h in range(HEADS):
                rows_ref[0, t, h * 8 : h * 8 + 6, :] = hi_ref[t, h * 6 : h * 6 + 6, :]
        for a in range(2):
            rows = joined(rows_ref.at[a])
            for b in range(2):
                chunk = (b * 2 + a) * 4 + zw
                expand_rows(rows, (1 - b) * HLON, chunk, wide_ref)
                tail = wide_ref[chunk, 2] + (pen_prev if a == 0 else pen_own)
                if zw == 3:
                    tail = tail + pen_z
                wide_ref[chunk, 2] = tail
    above = [prev_ref.at[2], prev_ref.at[0], prev_ref.at[1], prev_ref.at[3]]
    here = [[fl_ref.at[a], left_ref.at[a], right_ref.at[a], fr_ref.at[a]] for a in range(2)]
    below = [next_ref.at[2], next_ref.at[0], next_ref.at[1], next_ref.at[3]]
    for b in range(2):
        for a in range(2):
            pair = (above, here[0]) if a == 0 else (here[1], below)
            sources = [pair[part // 2][b * 2 + part % 2] for part in range(4)]
            items = []
            for zw in range(4):
                chunk = (b * 2 + a) * 4 + zw
                tokens = jnp.concatenate([src[zw].astype(F32) for src in sources], axis=0)
                normed = normalize(tokens, gain_one)
                keys = dot(normed, wk).astype(BF16)
                values = with_ones(dot(normed, wv))
                items.append(
                    (keys, values, q_ref[chunk * QP : (chunk + 1) * QP, :], joined(wide_ref.at[chunk]).astype(BF16))
                )
            for zw, out in enumerate(attend(items, select)):
                chunk = (b * 2 + a) * 4 + zw
                o_ref[chunk * QP : (chunk + 1) * QP, :] = out
    own_ref[...] = feed_forward(
        own_ref[...], o_ref[...].astype(BF16), gain_two, wproj_ref[0], wup_ref[0], wdown_ref[0]
    )
    for part in range(4):
        a, b = divmod(part, 2)
        for zw in range(4):
            at = ((b * 2 + a) * 4 + zw) * QP
            for t, tile in enumerate(tiles_of(own_ref[at : at + QB, :])):
                if zw < 3:
                    plain_ref[part, t, pl.ds(zw * QB + 18, QB), :] = tile
                else:
                    plain_ref[part, t, pl.ds(zw * QB + 18, 18), :] = tile[:18]
                    plain_ref[part, t, pl.ds(0, 18), :] = tile[18:]
    for r in range(WLAT):
        for o in range(WLON):
            part = r // HLAT * 2 + o // HLON
            at = (r % HLAT) * 6 + o % HLON
            out_ref[r, o] = whole_row(
                plain_ref[part, 0, pl.ds(at, Z, stride=18), :], plain_ref[part, 1, pl.ds(at, Z, stride=18), :]
            ).astype(BF16)


def whole(shape):
    return pl.BlockSpec(shape, lambda *_: (0,) * len(shape))


def picked(shape, layer):
    return pl.BlockSpec((1,) + shape[1:], lambda *_: (layer,) + (0,) * (len(shape) - 1))


def weight_specs(layer, gains, w_qkv, w_proj, w_up, w_down):
    return [whole(gains.shape)] + [picked(w.shape, layer) for w in (w_qkv, w_proj, w_up, w_down)]


PARAMS = pltpu.CompilerParams(vmem_limit_bytes=56 * 1024 * 1024)


def shifted(value, axis, steps):
    count = lax.axis_size(axis)
    pairs = [(source, (source + steps) % count) for source in range(count)]
    return lax.ppermute(value, axis, pairs)


def shards(grid, gains, w_qkv, w_proj, w_up, w_down, tables):
    grid = grid.transpose(1, 2, 0, 3)
    w_down = w_down.transpose(0, 2, 1)
    plain = jnp.asarray(key_select(False))
    masked = jnp.asarray(key_select(True))
    weights = (gains, w_qkv, w_proj, w_up, w_down)
    half = jax.ShapeDtypeStruct((2, 4, QP, C), BF16)
    tok = pltpu.VMEM((16 * QP, C), F32)
    plain_tok = pltpu.VMEM((4, 2, TSPAN, 128), F32)
    left, right, tabhi = pl.pallas_call(
        first_kernel,
        grid=(1,),
        in_specs=[whole(grid.shape)]
        + weight_specs(0, *weights)
        + [picked(tables.shape, 0), picked(tables.shape, 1)]
        + [whole(plain.shape)],
        out_specs=[whole(half.shape)] * 3,
        out_shape=[half, half, half],
        scratch_shapes=[
            plain_tok, tok, tok,
            pltpu.VMEM((2, TILES, 48, 128), F32),
            pltpu.VMEM((TILES, 4 * QP, 128), F32),
            pltpu.VMEM((16, TILES, QL, 128), F32),
        ],
        compiler_params=PARAMS,
        name="first_layer",
    )(grid, *weights, tables, tables, plain)
    from_left = shifted(right, "lon", 1)
    from_right = shifted(left, "lon", -1)
    down = jnp.concatenate([left[1:], right[1:], from_left[1:], from_right[1:], tabhi])
    up = jnp.concatenate([left[:1], right[:1], from_left[:1], from_right[:1]])
    from_prev = shifted(down, "lat", 1)
    from_next = shifted(up, "lat", -1)
    lat = lax.axis_index("lat")
    flags = jnp.stack([lat == 0, lat == lax.axis_size("lat") - 1]).astype(jnp.int32)
    moved = (left, right, from_left, from_right, from_prev, from_next)
    out = pl.pallas_call(
        second_kernel,
        grid=(1,),
        in_specs=[pl.BlockSpec(memory_space=pltpu.SMEM)]
        + [whole(m.shape) for m in moved]
        + weight_specs(1, *weights)
        + [picked(tables.shape, 1)]
        + [whole(masked.shape)],
        out_specs=whole(grid.shape),
        out_shape=jax.ShapeDtypeStruct(grid.shape, BF16),
        scratch_shapes=[
            plain_tok, tok, tok, tok,
            pltpu.VMEM((2, TILES, 48, 128), F32),
            pltpu.VMEM((TILES, QP, 128), F32),
            pltpu.VMEM((16, TILES, QL, 128), F32),
        ],
        compiler_params=PARAMS,
        name="second_layer",
    )(flags, *moved, *weights, tables, masked)
    return out.transpose(2, 0, 1, 3)


def solution(mesh):
    in_specs = (
        P(None, "lat", "lon", None),
        P(),
        P(),
        P(),
        P(),
        P(),
        P(None, None, "lat", None, None),
    )
    out_specs = P(None, "lat", "lon", None)
    return jax.shard_map(shards, mesh=mesh, in_specs=in_specs, out_specs=out_specs, check_vma=False)
```

time: 62.8 us -> 52.4 us (0.83)
  Pallas kernels: 27.5 us -> 19.4 us
  local copies, waits for them, and re-layouts: 10.2 us -> 6.24 us
  waiting for transfers between devices: 13 us -> 14.2 us
    pallas_call x1, Pallas kernels: 13.1 us -> 8.99 us  [shards(): pl.pallas_call(first_kernel, grid=(1,), in_specs=[whole(grid.shape)] + we...]
    pallas_call x1, Pallas kernels: 14.4 us -> 10.5 us  [shards(): pl.pallas_call(second_kernel, grid=(1,), in_specs=[pl.BlockSpec(memory_sp...]
    unnamed x19 -> x13, local copies, waits for them, and re-layouts: 7.29 us -> 5.23 us
    pallas_call x1 -> x0, local copies, waits for them, and re-layouts: 1.87 us -> none  [shards(): pl.pallas_call(second_kernel, grid=(1,), in_specs=[pl.BlockSpec(memory_sp...]
    ppermute x4, waiting for transfers between devices: 13 us -> 14.2 us  [shifted(): return lax.ppermute(value, axis, pairs)]
where the time goes in v1:
time: 52.4 us; the launch traced here: 52.1 us
  Pallas kernels  19.4 us (37%)
  waiting for transfers between devices  14.2 us (27%)
  starting transfers between devices  11.5 us (22%)
  local copies, waits for them, and re-layouts  6.24 us (12%)
  other arithmetic  0.67 us (1%)
    ppermute x4, waiting for transfers between devices, shifted(): return lax.ppermute(value, axis, pairs)  14.2 us
    ppermute x4, starting transfers between devices, shifted(): return lax.ppermute(value, axis, pairs)  11.5 us
    pallas_call x1, Pallas kernels, shards(): pl.pallas_call(second_kernel, grid=(1,), in_specs=[pl.BlockSpec(memory_sp...  10.5 us
    pallas_call x1, Pallas kernels, shards(): pl.pallas_call(first_kernel, grid=(1,), in_specs=[whole(grid.shape)] + we...  8.99 us
    unnamed x13, local copies, waits for them, and re-layouts  5.23 us
  transfers between devices with their start and end apart: 4, of which 2 were waited for; matrix products, arithmetic and copies ran while one was open for 3% of the time, Pallas kernels for 0%

profile of v1, /device:TPU:1, one launch (start us, length us, event | category | flops | bytes accessed | tf_op | source)
XLA Modules:
  0.0 52.1 jit_solution(14287531999527874724)
XLA Ops:
  0.0 2.1 %copy.10.tab_ref.tab1_ref = f32[2,4,1,6,3312]{4,3,2,1,0:T(8,128)} copy(f32[2,4,1,6,3312]{4,2,3,1,0:T(1,128)} %param.15) | data formatting | bytes 1271808 | tf_op args[6]
  2.1 9.0 %first_layer.1 = (bf16[2,4,40,192]{3,2,1,0:T(8,128)(2,1)}, bf16[2,4,40,192]{3,2,1,0:T(8,128)(2,1)}, bf16[2,4,40,192]{3,2,1,0:T(8,128)(2,1)}) custom-call(bf16[6,12,8,192]{3,2,1,0:T(8,128)(2,1)} %bitcast.7, f32[2,2,192]{2,1,0:T(2,128)} %gains_ref.3, bf16[2,192,576]{2,1,0:T(8,128)(2,1)} %wqkv_ref.3, bf16[2,192,192]{2,1,0:T(8,128)(2,1)} %wproj_ref.3, ...), custom_call_target="tpu_custom_call" | custom-call | tf_op jit(solution)/shard_map/first_layer/pallas_call | solution.py:338
  11.1 3.7 %collective-permute-start = (bf16[2,4,40,192]{3,2,1,0:T(8,128)(2,1)}, bf16[2,4,40,192]{3,2,1,0:T(8,128)(2,1)S(1)}, u32[]{:S(2)}, u32[]{:S(2)}) collective-permute-start(bf16[2,4,40,192]{3,2,1,0:T(8,128)(2,1)} %get-tuple-element.9.right_ref), channel_id=1, source_target_pairs={{0,16},{16,32},{32,48},{48,64},{64,80},{80,96},{96,112},{112,128},... | collective-permute-start | bytes 368648 | tf_op jit(solution)/shard_map/ppermute | solution.py:326
  14.8 0.0 copy-start
  14.8 5.4 %collective-permute-start.1 = (bf16[2,4,40,192]{3,2,1,0:T(8,128)(2,1)}, bf16[2,4,40,192]{3,2,1,0:T(8,128)(2,1)S(1)}, u32[]{:S(2)}, u32[]{:S(2)}) collective-permute-start(bf16[2,4,40,192]{3,2,1,0:T(8,128)(2,1)} %get-tuple-element.8.left_ref), channel_id=1, source_target_pairs={{0,240},{16,0},{32,16},{48,32},{64,48},{80,64},{96,80},{112,96},{1... | collective-permute-start | bytes 368648 | tf_op jit(solution)/shard_map/ppermute | solution.py:326
  20.2 1.0 %fusion = (bf16[1,4,40,192]{3,2,1,0:T(8,128)(2,1)S(1)}, bf16[6,4,40,192]{3,2,1,0:T(8,128)(2,1)S(1)}) fusion(bf16[2,4,40,192]{3,2,1,0:T(8,128)(2,1)} %get-tuple-element.8.left_ref), kind=kLoop, calls=%fused_computation.7 | loop fusion | bytes 286720 | tf_op jit(solution)/shard_map/slice | solution.py:359
  21.2 0.0 copy-done
  21.2 3.1 %collective-permute-done.fl_ref = bf16[2,4,40,192]{3,2,1,0:T(8,128)(2,1)S(1)} collective-permute-done((bf16[2,4,40,192]{3,2,1,0:T(8,128)(2,1)}, bf16[2,4,40,192]{3,2,1,0:T(8,128)(2,1)S(1)}, u32[]{:S(2)}, u32[]{:S(2)}) %collective-permute-start) | collective-permute-done | bytes 122912 | tf_op jit(solution)/shard_map/ppermute | solution.py:326
  24.3 0.0 copy-start.1
  24.3 0.6 %copy-done.1 = bf16[2,4,40,192]{3,2,1,0:T(8,128)(2,1)} copy-done((bf16[2,4,40,192]{3,2,1,0:T(8,128)(2,1)}, bf16[2,4,40,192]{3,2,1,0:T(8,128)(2,1)S(1)}, u32[]{:S(2)}) %copy-start.1) | copy-done | bytes 122904
  25.0 0.0 collective-permute-done.1.fr_ref
  25.0 0.0 copy-start.2
  25.0 0.0 copy-start.5
  25.0 0.6 %copy-done.2 = bf16[2,4,40,192]{3,2,1,0:T(8,128)(2,1)} copy-done((bf16[2,4,40,192]{3,2,1,0:T(8,128)(2,1)}, bf16[2,4,40,192]{3,2,1,0:T(8,128)(2,1)S(1)}, u32[]{:S(2)}) %copy-start.2) | copy-done | bytes 122904
  25.6 0.3 copy-done.5
  26.0 2.1 %collective-permute-start.2 = (bf16[6,4,40,192]{3,2,1,0:T(8,128)(2,1)S(1)}, bf16[6,4,40,192]{3,2,1,0:T(8,128)(2,1)S(1)}, u32[]{:S(2)}, u32[]{:S(2)}) collective-permute-start(bf16[6,4,40,192]{3,2,1,0:T(8,128)(2,1)S(1)} %constant_dynamic-update-slice_fusion), channel_id=1, source_target_pairs={{0,1},{1,2},{2,3},{3,4},{4,5},{5,6},{6,7},{7,8},{8,9},{9,10},{10,1... | collective-permute-start | bytes 1105928 | tf_op jit(solution)/shard_map/ppermute | solution.py:326
  28.0 0.1 pad_maximum_fusion
  28.1 0.3 collective-permute-start.3
  28.4 0.6 %add_convert_fusion.flags_ref = s32[2]{0:T(128)} fusion(pred[1]{0:T(512)(128)(4,1)} %bitcast.1, pred[1]{0:T(512)(128)(4,1)} %bitcast), kind=kLoop, calls=%fused_computation.6 | loop fusion | flops 4 | bytes 10 | tf_op jit(solution)/shard_map/convert_element_type | solution.py:363
  29.0 11.1 %collective-permute-done.3.next_ref = bf16[4,4,40,192]{3,2,1,0:T(8,128)(2,1)S(1)} collective-permute-done((bf16[4,4,40,192]{3,2,1,0:T(8,128)(2,1)S(1)}, bf16[4,4,40,192]{3,2,1,0:T(8,128)(2,1)S(1)}, u32[]{:S(2)}, u32[]{:S(2)}) %collective-permute-start.3) | collective-permute-done | bytes 245792 | tf_op jit(solution)/shard_map/ppermute | solution.py:326
  40.1 0.0 copy-start.4
  40.1 0.0 collective-permute-done.2.prev_ref
  40.1 0.7 %copy-done.4 = bf16[4,4,40,192]{3,2,1,0:T(8,128)(2,1)} copy-done((bf16[4,4,40,192]{3,2,1,0:T(8,128)(2,1)}, bf16[4,4,40,192]{3,2,1,0:T(8,128)(2,1)S(1)}, u32[]{:S(2)}) %copy-start.4) | copy-done | bytes 245784
  40.9 0.0 copy-start.3
  40.9 0.8 %copy-done.3 = bf16[6,4,40,192]{3,2,1,0:T(8,128)(2,1)} copy-done((bf16[6,4,40,192]{3,2,1,0:T(8,128)(2,1)}, bf16[6,4,40,192]{3,2,1,0:T(8,128)(2,1)S(1)}, u32[]{:S(2)}) %copy-start.3) | copy-done | bytes 368664
  41.7 10.5 %second_layer.1 = bf16[6,12,8,192]{3,2,1,0:T(8,128)(2,1)} custom-call(s32[2]{0:T(128)} %add_convert_fusion.flags_ref, bf16[2,4,40,192]{3,2,1,0:T(8,128)(2,1)} %get-tuple-element.8.left_ref, bf16[2,4,40,192]{3,2,1,0:T(8,128)(2,1)} %get-tuple-element.9.right_ref, bf16[2,4,40,192]{3,2,1,0:T(8,128)(2,1)} %copy-done.1, bf16[2,4,40,192]{3,2,1,0:T(8,128)(2,1)} %copy-done.2, ...), custom_call_target="tpu_custom_call" | custom-call | tf_op jit(solution)/shard_map/second_layer/pallas_call | solution.py:365
  (4 shorter events, 0.0 us)
Async XLA Ops:
  11.1 13.2 %collective-permute-start = (bf16[2,4,40,192]{3,2,1,0:T(8,128)(2,1)}, bf16[2,4,40,192]{3,2,1,0:T(8,128)(2,1)S(1)}, u32[]{:S(2)}, u32[]{:S(2)}) collective-permute-start(bf16[2,4,40,192]{3,2,1,0:T(8,128)(2,1)} %get-tuple-element.9.right_ref), channel_id=1, source_target_pairs={{0,16},{16,32},{32,48},{48,64},{64,80},{80,96},{96,112},{112,128},... | collective-permute-start | bytes 368648 | tf_op jit(solution)/shard_map/ppermute | solution.py:326
  14.8 6.4 %copy-start = (bf16[2,4,40,192]{3,2,1,0:T(8,128)(2,1)S(1)}, bf16[2,4,40,192]{3,2,1,0:T(8,128)(2,1)}, u32[]{:S(2)}) copy-start(bf16[2,4,40,192]{3,2,1,0:T(8,128)(2,1)} %get-tuple-element.9.right_ref) | copy-start | bytes 368644
  14.8 10.1 %collective-permute-start.1 = (bf16[2,4,40,192]{3,2,1,0:T(8,128)(2,1)}, bf16[2,4,40,192]{3,2,1,0:T(8,128)(2,1)S(1)}, u32[]{:S(2)}, u32[]{:S(2)}) collective-permute-start(bf16[2,4,40,192]{3,2,1,0:T(8,128)(2,1)} %get-tuple-element.8.left_ref), channel_id=1, source_target_pairs={{0,240},{16,0},{32,16},{48,32},{64,48},{80,64},{96,80},{112,96},{1... | collective-permute-start | bytes 368648 | tf_op jit(solution)/shard_map/ppermute | solution.py:326
  24.3 0.7 %copy-start.1 = (bf16[2,4,40,192]{3,2,1,0:T(8,128)(2,1)}, bf16[2,4,40,192]{3,2,1,0:T(8,128)(2,1)S(1)}, u32[]{:S(2)}) copy-start(bf16[2,4,40,192]{3,2,1,0:T(8,128)(2,1)S(1)} %collective-permute-done.fl_ref) | copy-start | bytes 368644
  25.0 0.7 %copy-start.2 = (bf16[2,4,40,192]{3,2,1,0:T(8,128)(2,1)}, bf16[2,4,40,192]{3,2,1,0:T(8,128)(2,1)S(1)}, u32[]{:S(2)}) copy-start(bf16[2,4,40,192]{3,2,1,0:T(8,128)(2,1)S(1)} %collective-permute-done.1.fr_ref) | copy-start | bytes 368644
  25.0 1.0 %copy-start.5 = (bf16[2,4,40,192]{3,2,1,0:T(8,128)(2,1)S(1)}, bf16[2,4,40,192]{3,2,1,0:T(8,128)(2,1)}, u32[]{:S(2)}) copy-start(bf16[2,4,40,192]{3,2,1,0:T(8,128)(2,1)} %get-tuple-element.10) | copy-start | bytes 368644
  26.0 14.2 %collective-permute-start.2 = (bf16[6,4,40,192]{3,2,1,0:T(8,128)(2,1)S(1)}, bf16[6,4,40,192]{3,2,1,0:T(8,128)(2,1)S(1)}, u32[]{:S(2)}, u32[]{:S(2)}) collective-permute-start(bf16[6,4,40,192]{3,2,1,0:T(8,128)(2,1)S(1)} %constant_dynamic-update-slice_fusion), channel_id=1, source_target_pairs={{0,1},{1,2},{2,3},{3,4},{4,5},{5,6},{6,7},{7,8},{8,9},{9,10},{10,1... | collective-permute-start | bytes 1105928 | tf_op jit(solution)/shard_map/ppermute | solution.py:326
  28.1 12.0 %collective-permute-start.3 = (bf16[4,4,40,192]{3,2,1,0:T(8,128)(2,1)S(1)}, bf16[4,4,40,192]{3,2,1,0:T(8,128)(2,1)S(1)}, u32[]{:S(2)}, u32[]{:S(2)}) collective-permute-start(bf16[4,4,40,192]{3,2,1,0:T(8,128)(2,1)S(1)} %pad_maximum_fusion), channel_id=1, source_target_pairs={{0,15},{1,0},{2,1},{3,2},{4,3},{5,4},{6,5},{7,6},{8,7},{9,8},{10,9... | collective-permute-start | bytes 737288 | tf_op jit(solution)/shard_map/ppermute | solution.py:326
  40.1 0.7 %copy-start.4 = (bf16[4,4,40,192]{3,2,1,0:T(8,128)(2,1)}, bf16[4,4,40,192]{3,2,1,0:T(8,128)(2,1)S(1)}, u32[]{:S(2)}) copy-start(bf16[4,4,40,192]{3,2,1,0:T(8,128)(2,1)S(1)} %collective-permute-done.3.next_ref) | copy-start | bytes 737284
  40.9 0.8 %copy-start.3 = (bf16[6,4,40,192]{3,2,1,0:T(8,128)(2,1)}, bf16[6,4,40,192]{3,2,1,0:T(8,128)(2,1)S(1)}, u32[]{:S(2)}) copy-start(bf16[6,4,40,192]{3,2,1,0:T(8,128)(2,1)S(1)} %collective-permute-done.2.prev_ref) | copy-start | bytes 1105924

commit v2 on v1

v2 whole, which is shorter than its diff:
```python
import functools
import math

import jax
import jax.numpy as jnp
import numpy as np
from jax import lax
from jax.experimental import pallas as pl
from jax.experimental.pallas import tpu as pltpu
from jax.sharding import PartitionSpec as P

C = 192
HEADS = 6
HEAD = 32
FF = 768
Z = 8
WZ = 2
WLAT = 6
WLON = 12
HLAT = 3
HLON = 6
SPAN = WZ * WLAT * WLON
QB = WZ * HLAT * HLON
QUAD = Z * HLAT * HLON
BAND = 2 * WLON - 1
TROW = WLAT * BAND
TW = 384
TILES = TW // 128
QP = 40
SP = 4 * QP
QL = HEADS * QP
PEN = 300
ONE = 330
TSPAN = 168

EPS = 1e-05
LOG2E = math.log2(math.e)
BIG = -1e30
F32 = jnp.float32
BF16 = jnp.bfloat16
NT = (((1,), (1,)), ((), ()))


def key_select(masked):
    sel = np.zeros((TW, SP), np.float32)
    for part in range(4):
        for zj in range(WZ):
            for r in range(HLAT):
                for o in range(HLON):
                    col = part * QP + zj * 18 + r * 6 + o
                    rj = part // 2 * HLAT + r
                    oj = part % 2 * HLON + o
                    sel[zj * TROW + rj * BAND + oj + WLON - 1, col] = 1
                    if masked:
                        sel[PEN + zj, col] = 1
                        sel[PEN + 2 + part // 2, col] = 1
        sel[ONE : ONE + WLON, part * QP + QB : (part + 1) * QP] = BIG
    return sel


def normalize(values, gain):
    mean = jnp.mean(values, axis=-1, keepdims=True)
    centered = values - mean
    var = jnp.mean(centered * centered, axis=-1, keepdims=True)
    return (centered * lax.rsqrt(var + EPS) * gain).astype(BF16)


def dot(a, b):
    return jnp.dot(a, b, preferred_element_type=F32)


def dot_nt(a, b):
    return lax.dot_general(a, b, NT, preferred_element_type=F32)


def table_rows(table, half, rows_ref):
    blank = jnp.zeros((HEADS, TW - 2 * TROW), F32)
    lane = lax.broadcasted_iota(jnp.int32, blank.shape, 1) + 2 * TROW
    blank = jnp.where(lane == ONE, 1.0, blank)
    for zi in range(WZ):
        for r in range(HLAT):
            at = [((zi * WZ + zj) * WLAT + half * HLAT + r) * TROW for zj in range(WZ)]
            wide = jnp.concatenate([table[:, k : k + TROW] for k in at] + [blank], axis=1)
            for t in range(TILES):
                rows_ref[t, pl.ds(zi * HLAT + r, HEADS, stride=8), :] = (
                    wide[:, t * 128 : (t + 1) * 128]
                )


def joined(tiles):
    return jnp.concatenate([tiles[t] for t in range(TILES)], axis=-1)


def expand_rows(rows, first, chunk, wide_ref):
    for o in range(HLON):
        shift = first + o
        rolled = pltpu.roll(rows, shift, 1) if shift else rows
        for h in range(HEADS):
            for t in range(TILES):
                wide_ref[chunk, t, pl.ds(h * QP + o, 6, stride=6), :] = (
                    rolled[h * 8 : h * 8 + 6, t * 128 : (t + 1) * 128]
                )


def head_lanes():
    lanes = lax.broadcasted_iota(jnp.int32, (1, C), 1)
    return [(lanes >= h * HEAD) & (lanes < (h + 1) * HEAD) for h in range(HEADS)]


def attend(items):
    own = head_lanes()
    stacks = [
        jnp.concatenate([jnp.where(own[h], q, 0.0) for h in range(HEADS)], axis=0).astype(BF16)
        for _, _, q, _ in items
    ]
    scores = [dot_nt(st, it[0]) + it[3]() for st, it in zip(stacks, items)]
    weights = [
        jnp.exp2(s - jnp.max(s, axis=1, keepdims=True)).astype(BF16) for s in scores
    ]
    mixed = [dot(p, it[1]) for p, it in zip(weights, items)]
    outs = []
    for m in mixed:
        scaled = m[:, :C] * (1.0 / m[:, C : C + 1])
        out = scaled[:QP]
        for h in range(1, HEADS):
            out = jnp.where(own[h], scaled[h * QP : (h + 1) * QP], out)
        outs.append(out)
    return outs


class Fetch:
    def __init__(self, sems):
        self.sems = sems
        self.copies = {}

    def start(self, name, source, target):
        copy = pltpu.make_async_copy(source, target, self.sems.at[len(self.copies)])
        self.copies[name] = copy
        copy.start()

    def wait(self, *names):
        for name in names:
            self.copies[name].wait()


def feed_forward(resid, mixed, gain_two, w_proj, w_up, w_down_t):
    first = (resid + dot(mixed, w_proj)).astype(BF16)
    first32 = first.astype(F32)
    inner = normalize(first32, gain_two)
    hidden = dot(inner, w_up)
    hidden = (hidden * 0.5 * (1.0 + lax.erf(hidden * (0.5**0.5)))).astype(BF16)
    return first32 + dot_nt(hidden, w_down_t)


QSCALE = HEAD**-0.5 * LOG2E


def with_ones(values):
    lanes = lax.broadcasted_iota(jnp.int32, values.shape, 1)
    return jnp.where(lanes == C, 1.0, values).astype(BF16)


def value_weights(qkv_ref):
    return jnp.concatenate([qkv_ref[:, 2 * C :], jnp.zeros((C, 256 - C), BF16)], axis=1)


def tiles_of(value):
    return value[:, :128], jnp.concatenate([value[:, 128:], value[:, 128:]], axis=1)


def whole_row(first, second):
    return jnp.concatenate([first, second[:, : C - 128]], axis=1)


def first_kernel(
    x_ref, gains_ref, wqkv_ref, wproj_ref, wup_ref, wdown_ref, tab_ref,
    select_ref,
    fast_ref, slow_ref,
    plain_ref, tok_ref, o_ref, rows_ref, wide_ref,
):
    plain_ref[...] = jnp.zeros_like(plain_ref)
    for r in range(WLAT):
        for o in range(WLON):
            part = r // HLAT * 2 + o // HLON
            at = (r % HLAT) * 6 + o % HLON
            for t, tile in enumerate(tiles_of(x_ref[r, o].astype(F32))):
                plain_ref[part, t, pl.ds(at, Z, stride=18), :] = tile
    for part in range(4):
        for w in range(4):
            rows = pl.ds(w * QB, QP)
            at = (part * 4 + w) * QP
            tok_ref[at : at + QP, :] = whole_row(plain_ref[part, 0, rows, :], plain_ref[part, 1, rows, :])
    select = select_ref[...].astype(BF16)
    for w in range(4):
        table = tab_ref[0, w, :, 0, :] * LOG2E
        for a in range(2):
            table_rows(table, a, rows_ref.at[a])
            rows = joined(rows_ref.at[a])
            for b in range(2):
                expand_rows(rows, b * HLON, w * 4 + a * 2 + b, wide_ref)
    gain_one = gains_ref[0, 0:1]
    gain_two = gains_ref[0, 1:2]
    wqk = wqkv_ref[0, :, : 2 * C]
    wv = value_weights(wqkv_ref.at[0])
    for w in range(4):
        tokens = jnp.concatenate(
            [tok_ref[(part * 4 + w) * QP : (part * 4 + w + 1) * QP, :] for part in range(4)], axis=0
        )
        normed = normalize(tokens, gain_one)
        both = dot(normed, wqk)
        query = both[:, :C] * QSCALE
        keys = both[:, C:].astype(BF16)
        values = with_ones(dot(normed, wv))
        items = [
            (keys, values, query[part * QP : (part + 1) * QP],
             lambda chunk=w * 4 + part: dot(joined(wide_ref.at[chunk]).astype(BF16), select))
            for part in range(4)
        ]
        for part, out in enumerate(attend(items)):
            o_ref[(part * 4 + w) * QP : (part * 4 + w + 1) * QP, :] = out
    tok_ref[...] = feed_forward(
        tok_ref[...], o_ref[...].astype(BF16), gain_two, wproj_ref[0], wup_ref[0], wdown_ref[0]
    )
    for part in range(4):
        for w in range(4):
            at = (part * 4 + w) * QP
            for t, tile in enumerate(tiles_of(tok_ref[at : at + QB, :])):
                plain_ref[part, t, pl.ds(w * QB, QB), :] = tile
                if w == 0:
                    plain_ref[part, t, pl.ds(QUAD, 18), :] = tile[:18]
    even = lax.axis_index("lon") % 2 == 0
    for a in range(2):
        for zw in range(4):
            rows = pl.ds(zw * QB + 18, QP)
            left, right = (
                whole_row(plain_ref[a * 2 + b, 0, rows, :], plain_ref[a * 2 + b, 1, rows, :]) for b in range(2)
            )
            fast_ref[a, zw] = jnp.where(even, right, left).astype(BF16)
            slow_ref[a, zw] = jnp.where(even, left, right).astype(BF16)


def bias_kernel(tab_ref, prev_tab_ref, select_ref, bias_ref, rows_ref, work_ref, tv_ref, sems):
    fetch = Fetch(sems)
    fetch.start("own", tab_ref.at[1], tv_ref.at[1])
    fetch.start("prev", prev_tab_ref.at[1], tv_ref.at[0])
    fetch.wait("own", "prev")
    select = select_ref[...].astype(BF16)
    lane = lax.broadcasted_iota(jnp.int32, (QL, 128), 1) + 256
    zi = (lax.broadcasted_iota(jnp.int32, (QL, 1), 0) % QP) // 18
    pen_z = jnp.where(((lane == PEN) & (zi == 1)) | ((lane == PEN + 1) & (zi == 0)), BIG, 0.0)
    lane_row = lane[:1]
    pens = (
        jnp.where((lane_row == PEN + 2) & (lax.axis_index("lat") == 0), BIG, 0.0),
        jnp.where((lane_row == PEN + 3) & (lax.axis_index("lat") == lax.axis_size("lat") - 1), BIG, 0.0),
    )
    for zw in range(4):
        for a in range(2):
            table_rows(tv_ref[a, zw, :, 0, :] * LOG2E, 1 - a, rows_ref.at[a])
            rows = joined(rows_ref.at[a])
            for b in range(2):
                slot = (zw % 2) * 4 + b * 2 + a
                expand_rows(rows, (1 - b) * HLON, slot, work_ref)
                tail = work_ref[slot, 2] + pens[a]
                if zw == 3:
                    tail = tail + pen_z
                wide = jnp.concatenate([work_ref[slot, 0], work_ref[slot, 1], tail], axis=1)
                bias_ref[(b * 2 + a) * 4 + zw] = dot(wide.astype(BF16), select).astype(BF16)


def second_kernel(
    fast_any, slow_any, from_fast_any, from_slow_any, lat_fast_any, lat_slow_any, bias_any,
    gains_ref, wqkv_any, wproj_any, wup_any, wdown_any,
    out_ref,
    plain_ref, own_ref, o_ref,
    near_ref, vert_ref, bias_ref,
    qkv_ref, proj_ref, up_ref, down_ref, sems,
):
    fetch = Fetch(sems)
    even = 1 - lax.axis_index("lon") % 2
    lat_even = 1 - lax.axis_index("lat") % 2
    columns = (1 + even, 2 - even, 3 * even, 3 - 3 * even)
    sides = (fast_any, slow_any, from_fast_any, from_slow_any)
    for i in range(2):
        fetch.start(f"near{i}", sides[i], near_ref.at[columns[i]])
    fetch.start("qkv", wqkv_any.at[1], qkv_ref)
    for i in range(2, 4):
        fetch.start(f"near{i}", sides[i], near_ref.at[columns[i]])
    for i in range(4):
        fetch.start(f"fast{i}", lat_fast_any.at[i], vert_ref.at[lat_even, columns[i]])
        fetch.start(f"slow{i}", lat_slow_any.at[i], vert_ref.at[1 - lat_even, columns[i]])
    fetch.start("bias", bias_any, bias_ref)
    fetch.start("proj", wproj_any.at[1], proj_ref)
    fetch.start("up", wup_any.at[1], up_ref)
    fetch.start("down", wdown_any.at[1], down_ref)
    gain_one = gains_ref[1, 0:1]
    gain_two = gains_ref[1, 1:2]
    fetch.wait("near0", "near1", "qkv")
    wq = qkv_ref[:, :C]
    wk = qkv_ref[:, C : 2 * C]
    wv = value_weights(qkv_ref)
    for b in range(2):
        for a in range(2):
            for zw in range(4):
                at = ((b * 2 + a) * 4 + zw) * QP
                own_ref[at : at + QP, :] = near_ref[1 + b, a, zw].astype(F32)
    query = dot(normalize(own_ref[...], gain_one), wq) * QSCALE
    fetch.wait("near2", "near3", "bias")
    fetch.wait(*[f"{kind}{i}" for kind in ("fast", "slow") for i in range(4)])
    above = [vert_ref.at[0, i] for i in range(4)]
    here = [[near_ref.at[i, a] for i in range(4)] for a in range(2)]
    below = [vert_ref.at[1, i] for i in range(4)]
    for b in range(2):
        for a in range(2):
            pair = (above, here[0]) if a == 0 else (here[1], below)
            sources = [pair[part // 2][b * 2 + part % 2] for part in range(4)]
            items = []
            for zw in range(4):
                chunk = (b * 2 + a) * 4 + zw
                tokens = jnp.concatenate([src[zw].astype(F32) for src in sources], axis=0)
                normed = normalize(tokens, gain_one)
                keys = dot(normed, wk).astype(BF16)
                values = with_ones(dot(normed, wv))
                items.append(
                    (keys, values, query[chunk * QP : (chunk + 1) * QP],
                     lambda chunk=chunk: bias_ref[chunk].astype(F32))
                )
            for zw, out in enumerate(attend(items)):
                chunk = (b * 2 + a) * 4 + zw
                o_ref[chunk * QP : (chunk + 1) * QP, :] = out
    fetch.wait("proj", "up", "down")
    own_ref[...] = feed_forward(
        own_ref[...], o_ref[...].astype(BF16), gain_two, proj_ref[...], up_ref[...], down_ref[...]
    )
    for part in range(4):
        a, b = divmod(part, 2)
        for zw in range(4):
            at = ((b * 2 + a) * 4 + zw) * QP
            for t, tile in enumerate(tiles_of(own_ref[at : at + QB, :])):
                if zw < 3:
                    plain_ref[part, t, pl.ds(zw * QB + 18, QB), :] = tile
                else:
                    plain_ref[part, t, pl.ds(zw * QB + 18, 18), :] = tile[:18]
                    plain_ref[part, t, pl.ds(0, 18), :] = tile[18:]
    for r in range(WLAT):
        for o in range(WLON):
            part = r // HLAT * 2 + o // HLON
            at = (r % HLAT) * 6 + o % HLON
            out_ref[r, o] = whole_row(
                plain_ref[part, 0, pl.ds(at, Z, stride=18), :], plain_ref[part, 1, pl.ds(at, Z, stride=18), :]
            ).astype(BF16)


def whole(shape):
    return pl.BlockSpec(shape, lambda *_: (0,) * len(shape))


ANY = pl.BlockSpec(memory_space=pl.ANY)


def picked(shape, layer):
    return pl.BlockSpec((1,) + shape[1:], lambda *_: (layer,) + (0,) * (len(shape) - 1))


def weight_specs(layer, gains, w_qkv, w_proj, w_up, w_down):
    return [whole(gains.shape)] + [picked(w.shape, layer) for w in (w_qkv, w_proj, w_up, w_down)]


PARAMS = pltpu.CompilerParams(vmem_limit_bytes=56 * 1024 * 1024)


def shifted(value, axis, steps):
    count = lax.axis_size(axis)
    pairs = [(source, (source + steps) % count) for source in range(count)]
    return lax.ppermute(value, axis, pairs)


def paired(axis, first):
    count = lax.axis_size(axis)
    return [(i, (i + 1 if (i + first) % 2 == 0 else i - 1) % count) for i in range(count)]


def call(kernel, name, in_specs, outs, scratch, args):
    single = not isinstance(outs, list)
    specs = [whole(o.shape) for o in (outs if not single else [outs])]
    return pl.pallas_call(
        kernel,
        grid=(1,),
        in_specs=in_specs,
        out_specs=specs[0] if single else specs,
        out_shape=outs,
        scratch_shapes=scratch,
        compiler_params=PARAMS,
        name=name,
    )(*args)


def shards(grid, gains, w_qkv, w_proj, w_up, w_down, tables):
    grid = grid.transpose(1, 2, 0, 3)
    w_down = w_down.transpose(0, 2, 1)
    tables = tables.transpose(0, 1, 3, 2, 4)
    prev_tables = shifted(tables, "lat", 1)
    plain = jnp.asarray(key_select(False))
    masked = jnp.asarray(key_select(True))
    weights = (gains, w_qkv, w_proj, w_up, w_down)
    half = jax.ShapeDtypeStruct((2, 4, QP, C), BF16)
    tok = pltpu.VMEM((16 * QP, C), F32)
    plain_tok = pltpu.VMEM((4, 2, TSPAN, 128), F32)
    table_work = pltpu.VMEM((2, TILES, 48, 128), F32)
    weight_mem = [pltpu.VMEM(w.shape[1:], BF16) for w in weights[1:]]
    fast, slow = call(
        first_kernel, "first_layer",
        [whole(grid.shape)] + weight_specs(0, *weights) + [picked(tables.shape, 0), whole(plain.shape)],
        [half, half],
        [plain_tok, tok, tok, table_work, pltpu.VMEM((16, TILES, QL, 128), F32)],
        (grid, *weights, tables, plain),
    )
    from_fast = lax.ppermute(fast, "lon", paired("lon", 0))
    from_slow = lax.ppermute(slow, "lon", paired("lon", 1))
    from_fast, from_slow, prev_tables = lax.optimization_barrier((from_fast, from_slow, prev_tables))
    bias = call(
        bias_kernel, "second_bias",
        [ANY, ANY, whole(masked.shape)],
        jax.ShapeDtypeStruct((16, QL, SP), BF16),
        [table_work, pltpu.VMEM((8, TILES, QL, 128), F32),
         pltpu.VMEM((2,) + tables.shape[1:], F32), pltpu.SemaphoreType.DMA((2,))],
        (tables, prev_tables, masked),
    )
    odd = lax.axis_index("lat") % 2
    sides = (fast, slow, from_fast, from_slow)
    toward_fast = jnp.concatenate([lax.dynamic_slice_in_dim(v, 1 - odd, 1, 0) for v in sides])
    toward_slow = jnp.concatenate([lax.dynamic_slice_in_dim(v, odd, 1, 0) for v in sides])
    lat_fast = lax.ppermute(toward_fast, "lat", paired("lat", 0))
    lat_slow = lax.ppermute(toward_slow, "lat", paired("lat", 1))
    moved = (*sides, lat_fast, lat_slow, bias)
    out = call(
        second_kernel, "second_layer",
        [ANY] * 7 + [whole(gains.shape)] + [ANY] * 4,
        jax.ShapeDtypeStruct(grid.shape, BF16),
        [plain_tok, tok, tok]
        + [pltpu.VMEM((4,) + half.shape, BF16), pltpu.VMEM((2, 4) + half.shape[1:], BF16), pltpu.VMEM(bias.shape, BF16)]
        + weight_mem + [pltpu.SemaphoreType.DMA((17,))],
        (*moved, *weights),
    )
    return out.transpose(2, 0, 1, 3)


def solution(mesh):
    in_specs = (
        P(None, "lat", "lon", None),
        P(),
        P(),
        P(),
        P(),
        P(),
        P(None, None, "lat", None, None),
    )
    out_specs = P(None, "lat", "lon", None)
    return jax.shard_map(shards, mesh=mesh, in_specs=in_specs, out_specs=out_specs, check_vma=False)
```

time: 52.4 us -> 43.5 us (0.83)
  waiting for transfers between devices: 14.2 us -> 4.84 us
  local copies, waits for them, and re-layouts: 6.24 us -> 1.79 us
  Pallas kernels: 19.4 us -> 23.3 us
  starting transfers between devices: 11.5 us -> 13 us
    ppermute x4 -> x1, waiting for transfers between devices: 14.2 us -> 0.01 us  [shifted(): return lax.ppermute(value, axis, pairs)]
    ppermute x0 -> x4, starting transfers between devices: none -> 10.3 us  [the longest x1 5.64 us: shards(): from_slow = lax.ppermute(slow, 'lon', paired('lon', 1))]
    ppermute x4 -> x1, starting transfers between devices: 11.5 us -> 2.69 us  [shifted(): return lax.ppermute(value, axis, pairs)]
    ppermute x0 -> x4, waiting for transfers between devices: none -> 4.84 us  [the longest x1 2.18 us: shards(): from_slow = lax.ppermute(slow, 'lon', paired('lon', 1))]
    unnamed x13 -> x10, local copies, waits for them, and re-layouts: 5.23 us -> 0.74 us
    pallas_call x2 -> x3, Pallas kernels: 19.4 us -> 23.3 us  [call(): pl.pallas_call(kernel, grid=(1,), in_specs=in_specs, out_specs=specs[0] i...]
    dynamic_slice x0 -> x2, local copies, waits for them, and re-layouts: none -> 1.05 us  [shards(): lax.dynamic_slice_in_dim(v, odd, 1, 0)]
    slice x4 -> x0, local copies, waits for them, and re-layouts: 1.01 us -> none  [shards(): up = jnp.concatenate([left[:1], right[:1], from_left[:1], from_right[:1]])]
  transfers between devices with their start and end apart: 4 -> 5, of which waited for: 2 -> 3; matrix products, arithmetic and copies ran while one was open for 3% -> 3% of each run, Pallas kernels for 0% -> 34%
where the time goes in v2:
time: 43.5 us; the launch traced here: 43.3 us
  Pallas kernels  23.3 us (54%)
  starting transfers between devices  13 us (30%)
  waiting for transfers between devices  4.84 us (11%)
  local copies, waits for them, and re-layouts  1.79 us (4%)
    pallas_call x3, Pallas kernels, call(): pl.pallas_call(kernel, grid=(1,), in_specs=in_specs, out_specs=specs[0] i...  23.3 us
    ppermute x1, starting transfers between devices, shards(): from_slow = lax.ppermute(slow, 'lon', paired('lon', 1))  5.64 us
    ppermute x1, starting transfers between devices, shifted(): return lax.ppermute(value, axis, pairs)  2.69 us
    ppermute x1, starting transfers between devices, shards(): from_fast = lax.ppermute(fast, 'lon', paired('lon', 0))  2.62 us
    ppermute x1, waiting for transfers between devices, shards(): from_slow = lax.ppermute(slow, 'lon', paired('lon', 1))  2.18 us
    ppermute x1, starting transfers between devices, shards(): lat_slow = lax.ppermute(toward_slow, 'lat', paired('lat', 1))  1.92 us
    ppermute x1, waiting for transfers between devices, shards(): lat_slow = lax.ppermute(toward_slow, 'lat', paired('lat', 1))  1.9 us
    dynamic_slice x2, local copies, waits for them, and re-layouts, shards(): lax.dynamic_slice_in_dim(v, odd, 1, 0)  1.05 us
  transfers between devices with their start and end apart: 5, of which 3 were waited for; matrix products, arithmetic and copies ran while one was open for 3% of the time, Pallas kernels for 34%

profile of v2, /device:TPU:1, one launch (start us, length us, event | category | flops | bytes accessed | tf_op | source)
XLA Modules:
  0.0 43.3 jit_solution(16184999325449073984)
XLA Ops:
  0.0 2.7 %collective-permute-start.2 = (f32[2,4,6,1,3312]{4,3,2,1,0:T(1,128)}, f32[2,4,6,1,3312]{4,3,2,1,0:T(1,128)S(1)}, u32[]{:S(2)}, u32[]{:S(2)}) collective-permute-start(f32[2,4,6,1,3312]{4,3,2,1,0:T(1,128)} %bitcast.4), channel_id=1, source_target_pairs={{0,1},{1,2},{2,3},{3,4},{4,5},{5,6},{6,7},{7,8},{8,9},{9,10},{10,1... | collective-permute-start | bytes 1907720 | tf_op jit(solution)/shard_map/ppermute | solution.py:374
  2.7 8.5 %first_layer.1 = (bf16[2,4,40,192]{3,2,1,0:T(8,128)(2,1)}, bf16[2,4,40,192]{3,2,1,0:T(8,128)(2,1)}) custom-call(bf16[6,12,8,192]{3,2,1,0:T(8,128)(2,1)} %bitcast.9, f32[2,2,192]{2,1,0:T(2,128)} %gains_ref.3, bf16[2,192,576]{2,1,0:T(8,128)(2,1)} %wqkv_any.1, bf16[2,192,192]{2,1,0:T(8,128)(2,1)} %wproj_any.1, bf16[2,192,768]{2,1,0:T(8,128)(2,1)} %wup_any.1, ...), custom_call_target="tpu_custom_call" | custom-call | tf_op jit(solution)/shard_map/first_layer/pallas_call | solution.py:385
  11.2 2.6 %collective-permute-start = (bf16[2,4,40,192]{3,2,1,0:T(8,128)(2,1)}, bf16[2,4,40,192]{3,2,1,0:T(8,128)(2,1)S(1)}, u32[]{:S(2)}, u32[]{:S(2)}) collective-permute-start(bf16[2,4,40,192]{3,2,1,0:T(8,128)(2,1)} %get-tuple-element.10.fast_any), channel_id=1, source_target_pairs={{0,16},{16,0},{32,48},{48,32},{64,80},{80,64},{96,112},{112,96},{1... | collective-permute-start | bytes 368648 | tf_op jit(solution)/shard_map/ppermute | solution.py:417
  13.8 5.6 %collective-permute-start.1 = (bf16[2,4,40,192]{3,2,1,0:T(8,128)(2,1)}, bf16[2,4,40,192]{3,2,1,0:T(8,128)(2,1)S(1)}, u32[]{:S(2)}, u32[]{:S(2)}) collective-permute-start(bf16[2,4,40,192]{3,2,1,0:T(8,128)(2,1)} %get-tuple-element.11.slow_any), channel_id=1, source_target_pairs={{0,240},{16,32},{32,16},{48,64},{64,48},{80,96},{96,80},{112,128},... | collective-permute-start | bytes 368648 | tf_op jit(solution)/shard_map/ppermute | solution.py:418
  19.5 1.0 %constant_dynamic-slice_fusion.2 = (bf16[1,4,40,192]{3,2,1,0:T(8,128)(2,1)S(1)}, bf16[1,4,40,192]{3,2,1,0:T(8,128)(2,1)S(1)}, bf16[1,4,40,192]{3,2,1,0:T(8,128)(2,1)S(1)}, bf16[1,4,40,192]{3,2,1,0:T(8,128)(2,1)S(1)}) fusion(bf16[2,4,40,192]{3,2,1,0:T(8,128)(2,1)} %get-tuple-element.11.slow_any, s32[]{:T(128)S(6)} %select_n.21, s32[]{:T(128)S(6)} %select_n.20, ...), kind=kLoop, calls=%fused_computation.4 | loop fusion | bytes 491528 | tf_op jit(solution)/shard_map/dynamic_slice | solution.py:431
  20.5 0.8 %collective-permute-done.from_fast_any = bf16[2,4,40,192]{3,2,1,0:T(8,128)(2,1)S(1)} collective-permute-done((bf16[2,4,40,192]{3,2,1,0:T(8,128)(2,1)}, bf16[2,4,40,192]{3,2,1,0:T(8,128)(2,1)S(1)}, u32[]{:S(2)}, u32[]{:S(2)}) %collective-permute-start) | collective-permute-done | bytes 122912 | tf_op jit(solution)/shard_map/ppermute | solution.py:417
  21.3 0.0 copy-start
  21.3 2.2 %collective-permute-done.1.from_slow_any = bf16[2,4,40,192]{3,2,1,0:T(8,128)(2,1)S(1)} collective-permute-done((bf16[2,4,40,192]{3,2,1,0:T(8,128)(2,1)}, bf16[2,4,40,192]{3,2,1,0:T(8,128)(2,1)S(1)}, u32[]{:S(2)}, u32[]{:S(2)}) %collective-permute-start.1) | collective-permute-done | bytes 122912 | tf_op jit(solution)/shard_map/ppermute | solution.py:418
  23.4 0.0 copy-start.1
  23.4 0.0 collective-permute-done.2.prev_tab_ref
  23.5 0.0 copy-start.2
  23.5 0.1 pad_maximum_fusion
  23.6 0.1 collective-permute-start.3
  23.7 0.1 pad_maximum_fusion.1
  23.8 1.9 %collective-permute-start.4 = (bf16[4,4,40,192]{3,2,1,0:T(8,128)(2,1)S(1)}, bf16[4,4,40,192]{3,2,1,0:T(8,128)(2,1)S(1)}, u32[]{:S(2)}, u32[]{:S(2)}) collective-permute-start(bf16[4,4,40,192]{3,2,1,0:T(8,128)(2,1)S(1)} %pad_maximum_fusion.1), channel_id=1, source_target_pairs={{0,15},{1,2},{2,1},{3,4},{4,3},{5,6},{6,5},{7,8},{8,7},{9,10},{10,... | collective-permute-start | bytes 737288 | tf_op jit(solution)/shard_map/ppermute | solution.py:433
  25.7 0.0 copy-done.2
  25.7 6.4 %second_bias.1.bias_any = bf16[16,240,160]{2,1,0:T(8,128)(2,1)} custom-call(f32[2,4,6,1,3312]{4,3,2,1,0:T(1,128)} %bitcast.6, f32[2,4,6,1,3312]{4,3,2,1,0:T(1,128)} %copy-done.2, f32[384,160]{1,0:T(8,128)} %constant.26.clone.select_ref), custom_call_target="tpu_custom_call" | custom-call | tf_op jit(solution)/shard_map/second_bias/pallas_call | solution.py:385
  32.1 0.0 copy-done
  32.1 0.0 copy-done.1
  32.1 0.0 collective-permute-done.3.lat_fast_any
  32.1 0.0 copy-start.3
  32.1 1.9 %collective-permute-done.4.lat_slow_any = bf16[4,4,40,192]{3,2,1,0:T(8,128)(2,1)S(1)} collective-permute-done((bf16[4,4,40,192]{3,2,1,0:T(8,128)(2,1)S(1)}, bf16[4,4,40,192]{3,2,1,0:T(8,128)(2,1)S(1)}, u32[]{:S(2)}, u32[]{:S(2)}) %collective-permute-start.4) | collective-permute-done | bytes 245792 | tf_op jit(solution)/shard_map/ppermute | solution.py:433
  34.0 0.0 copy-done.3
  34.0 0.0 copy-start.4
  34.0 0.7 %copy-done.4 = bf16[4,4,40,192]{3,2,1,0:T(8,128)(2,1)} copy-done((bf16[4,4,40,192]{3,2,1,0:T(8,128)(2,1)}, bf16[4,4,40,192]{3,2,1,0:T(8,128)(2,1)S(1)}, u32[]{:S(2)}) %copy-start.4) | copy-done | bytes 245784
  34.8 8.4 %second_layer.1 = bf16[6,12,8,192]{3,2,1,0:T(8,128)(2,1)} custom-call(bf16[2,4,40,192]{3,2,1,0:T(8,128)(2,1)} %get-tuple-element.10.fast_any, bf16[2,4,40,192]{3,2,1,0:T(8,128)(2,1)} %get-tuple-element.11.slow_any, bf16[2,4,40,192]{3,2,1,0:T(8,128)(2,1)} %copy-done, bf16[2,4,40,192]{3,2,1,0:T(8,128)(2,1)} %copy-done.1, bf16[4,4,40,192]{3,2,1,0:T(8,128)(2,1)} %copy-done.3, ...), custom_call_target="tpu_custom_call" | custom-call | tf_op jit(solution)/shard_map/second_layer/pallas_call | solution.py:385
  (1 shorter events, 0.0 us)
Async XLA Ops:
  0.0 23.5 %collective-permute-start.2 = (f32[2,4,6,1,3312]{4,3,2,1,0:T(1,128)}, f32[2,4,6,1,3312]{4,3,2,1,0:T(1,128)S(1)}, u32[]{:S(2)}, u32[]{:S(2)}) collective-permute-start(f32[2,4,6,1,3312]{4,3,2,1,0:T(1,128)} %bitcast.4), channel_id=1, source_target_pairs={{0,1},{1,2},{2,3},{3,4},{4,5},{5,6},{6,7},{7,8},{8,9},{9,10},{10,1... | collective-permute-start | bytes 1907720 | tf_op jit(solution)/shard_map/ppermute | solution.py:374
  11.2 10.0 %collective-permute-start = (bf16[2,4,40,192]{3,2,1,0:T(8,128)(2,1)}, bf16[2,4,40,192]{3,2,1,0:T(8,128)(2,1)S(1)}, u32[]{:S(2)}, u32[]{:S(2)}) collective-permute-start(bf16[2,4,40,192]{3,2,1,0:T(8,128)(2,1)} %get-tuple-element.10.fast_any), channel_id=1, source_target_pairs={{0,16},{16,0},{32,48},{48,32},{64,80},{80,64},{96,112},{112,96},{1... | collective-permute-start | bytes 368648 | tf_op jit(solution)/shard_map/ppermute | solution.py:417
  13.8 9.6 %collective-permute-start.1 = (bf16[2,4,40,192]{3,2,1,0:T(8,128)(2,1)}, bf16[2,4,40,192]{3,2,1,0:T(8,128)(2,1)S(1)}, u32[]{:S(2)}, u32[]{:S(2)}) collective-permute-start(bf16[2,4,40,192]{3,2,1,0:T(8,128)(2,1)} %get-tuple-element.11.slow_any), channel_id=1, source_target_pairs={{0,240},{16,32},{32,16},{48,64},{64,48},{80,96},{96,80},{112,128},... | collective-permute-start | bytes 368648 | tf_op jit(solution)/shard_map/ppermute | solution.py:418
  21.3 10.8 %copy-start = (bf16[2,4,40,192]{3,2,1,0:T(8,128)(2,1)}, bf16[2,4,40,192]{3,2,1,0:T(8,128)(2,1)S(1)}, u32[]{:S(2)}) copy-start(bf16[2,4,40,192]{3,2,1,0:T(8,128)(2,1)S(1)} %collective-permute-done.from_fast_any) | copy-start | bytes 368644
  23.4 8.7 %copy-start.1 = (bf16[2,4,40,192]{3,2,1,0:T(8,128)(2,1)}, bf16[2,4,40,192]{3,2,1,0:T(8,128)(2,1)S(1)}, u32[]{:S(2)}) copy-start(bf16[2,4,40,192]{3,2,1,0:T(8,128)(2,1)S(1)} %collective-permute-done.1.from_slow_any) | copy-start | bytes 368644
  23.5 2.2 %copy-start.2 = (f32[2,4,6,1,3312]{4,3,2,1,0:T(1,128)}, f32[2,4,6,1,3312]{4,3,2,1,0:T(1,128)S(1)}, u32[]{:S(2)}) copy-start(f32[2,4,6,1,3312]{4,3,2,1,0:T(1,128)S(1)} %collective-permute-done.2.prev_tab_ref) | copy-start | bytes 1907716
  23.6 8.6 %collective-permute-start.3 = (bf16[4,4,40,192]{3,2,1,0:T(8,128)(2,1)S(1)}, bf16[4,4,40,192]{3,2,1,0:T(8,128)(2,1)S(1)}, u32[]{:S(2)}, u32[]{:S(2)}) collective-permute-start(bf16[4,4,40,192]{3,2,1,0:T(8,128)(2,1)S(1)} %pad_maximum_fusion), channel_id=1, source_target_pairs={{0,1},{1,0},{2,3},{3,2},{4,5},{5,4},{6,7},{7,6},{8,9},{9,8},{10,11... | collective-permute-start | bytes 737288 | tf_op jit(solution)/shard_map/ppermute | solution.py:432
  23.8 10.3 %collective-permute-start.4 = (bf16[4,4,40,192]{3,2,1,0:T(8,128)(2,1)S(1)}, bf16[4,4,40,192]{3,2,1,0:T(8,128)(2,1)S(1)}, u32[]{:S(2)}, u32[]{:S(2)}) collective-permute-start(bf16[4,4,40,192]{3,2,1,0:T(8,128)(2,1)S(1)} %pad_maximum_fusion.1), channel_id=1, source_target_pairs={{0,15},{1,2},{2,1},{3,4},{4,3},{5,6},{6,5},{7,8},{8,7},{9,10},{10,... | collective-permute-start | bytes 737288 | tf_op jit(solution)/shard_map/ppermute | solution.py:433
  32.1 1.9 %copy-start.3 = (bf16[4,4,40,192]{3,2,1,0:T(8,128)(2,1)}, bf16[4,4,40,192]{3,2,1,0:T(8,128)(2,1)S(1)}, u32[]{:S(2)}) copy-start(bf16[4,4,40,192]{3,2,1,0:T(8,128)(2,1)S(1)} %collective-permute-done.3.lat_fast_any) | copy-start | bytes 737284
  34.0 0.7 %copy-start.4 = (bf16[4,4,40,192]{3,2,1,0:T(8,128)(2,1)}, bf16[4,4,40,192]{3,2,1,0:T(8,128)(2,1)S(1)}, u32[]{:S(2)}) copy-start(bf16[4,4,40,192]{3,2,1,0:T(8,128)(2,1)S(1)} %collective-permute-done.4.lat_slow_any) | copy-start | bytes 737284

commit v3 on v2

--- a/solution.py
+++ b/solution.py
@@ -229,14 +229,26 @@
                 if w == 0:
                     plain_ref[part, t, pl.ds(QUAD, 18), :] = tile[:18]
     even = lax.axis_index("lon") % 2 == 0
+    low = lax.broadcasted_iota(jnp.int32, (QP, 128), 1) < 128 - (C - 128)
     for a in range(2):
-        for zw in range(4):
-            rows = pl.ds(zw * QB + 18, QP)
-            left, right = (
-                whole_row(plain_ref[a * 2 + b, 0, rows, :], plain_ref[a * 2 + b, 1, rows, :]) for b in range(2)
-            )
-            fast_ref[a, zw] = jnp.where(even, right, left).astype(BF16)
-            slow_ref[a, zw] = jnp.where(even, left, right).astype(BF16)
+        for pair in range(2):
+            rows = [pl.ds((pair * 2 + k) * QB + 18, QP) for k in range(2)]
+            sides = []
+            for b in range(2):
+                part = a * 2 + b
+                lasts = [plain_ref[part, 1, r, :] for r in rows]
+                sides.append([plain_ref[part, 0, r, :] for r in rows] + [jnp.where(low, lasts[0], lasts[1])])
+            for k, (left, right) in enumerate(zip(*sides)):
+                fast_ref[a, pair * 3 + k] = jnp.where(even, right, left).astype(BF16)
+                slow_ref[a, pair * 3 + k] = jnp.where(even, left, right).astype(BF16)
+
+
+def block_of(tiles_ref, zw):
+    pair, second = divmod(zw, 2)
+    last = tiles_ref[pair * 3 + 2].astype(F32)
+    if second:
+        last = pltpu.roll(last, 64, 1)
+    return whole_row(tiles_ref[pair * 3 + second].astype(F32), last)
 
 
 def bias_kernel(tab_ref, prev_tab_ref, select_ref, bias_ref, rows_ref, work_ref, tv_ref, sems):
@@ -302,7 +314,7 @@
         for a in range(2):
             for zw in range(4):
                 at = ((b * 2 + a) * 4 + zw) * QP
-                own_ref[at : at + QP, :] = near_ref[1 + b, a, zw].astype(F32)
+                own_ref[at : at + QP, :] = block_of(near_ref.at[1 + b, a], zw)
     query = dot(normalize(own_ref[...], gain_one), wq) * QSCALE
     fetch.wait("near2", "near3", "bias")
     fetch.wait(*[f"{kind}{i}" for kind in ("fast", "slow") for i in range(4)])
@@ -316,7 +328,7 @@
             items = []
             for zw in range(4):
                 chunk = (b * 2 + a) * 4 + zw
-                tokens = jnp.concatenate([src[zw].astype(F32) for src in sources], axis=0)
+                tokens = jnp.concatenate([block_of(src, zw) for src in sources], axis=0)
                 normed = normalize(tokens, gain_one)
                 keys = dot(normed, wk).astype(BF16)
                 values = with_ones(dot(normed, wv))
@@ -402,7 +414,7 @@
     plain = jnp.asarray(key_select(False))
     masked = jnp.asarray(key_select(True))
     weights = (gains, w_qkv, w_proj, w_up, w_down)
-    half = jax.ShapeDtypeStruct((2, 4, QP, C), BF16)
+    half = jax.ShapeDtypeStruct((2, 6, QP, 128), BF16)
     tok = pltpu.VMEM((16 * QP, C), F32)
     plain_tok = pltpu.VMEM((4, 2, TSPAN, 128), F32)
     table_work = pltpu.VMEM((2, TILES, 48, 128), F32)

time: 43.5 us -> 42.5 us (0.977)
  waiting for transfers between devices: 4.84 us -> 2.3 us
  Pallas kernels: 23.3 us -> 24.4 us
    ppermute x1, waiting for transfers between devices: 1.9 us -> 0.16 us  [shards(): lat_slow = lax.ppermute(toward_slow, 'lat', paired('lat', 1))]
    pallas_call x3, Pallas kernels: 23.3 us -> 24.4 us  [call(): pl.pallas_call(kernel, grid=(1,), in_specs=in_specs, out_specs=specs[0] i...]
    ppermute x1, waiting for transfers between devices: 0.75 us -> 0.01 us  [shards(): from_fast = lax.ppermute(fast, 'lon', paired('lon', 0))]
    unnamed x10, local copies, waits for them, and re-layouts: 0.74 us -> 1.25 us
  transfers between devices with their start and end apart: 5 -> 5, of which waited for: 3 -> 2; matrix products, arithmetic and copies ran while one was open for 3% -> 2% of each run, Pallas kernels for 34% -> 35%
where the time goes in v3:
time: 42.5 us; the launch traced here: 42.2 us
  Pallas kernels  24.4 us (57%)
  starting transfers between devices  13 us (31%)
  waiting for transfers between devices  2.3 us (5%)
  local copies, waits for them, and re-layouts  2.22 us (5%)
    pallas_call x3, Pallas kernels, call(): pl.pallas_call(kernel, grid=(1,), in_specs=in_specs, out_specs=specs[0] i...  24.4 us
    ppermute x1, starting transfers between devices, shards(): from_slow = lax.ppermute(slow, 'lon', paired('lon', 1))  5.63 us
    ppermute x1, starting transfers between devices, shifted(): return lax.ppermute(value, axis, pairs)  2.69 us
    ppermute x1, starting transfers between devices, shards(): from_fast = lax.ppermute(fast, 'lon', paired('lon', 0))  2.63 us
    ppermute x1, waiting for transfers between devices, shards(): from_slow = lax.ppermute(slow, 'lon', paired('lon', 1))  2.13 us
    ppermute x1, starting transfers between devices, shards(): lat_slow = lax.ppermute(toward_slow, 'lat', paired('lat', 1))  1.91 us
    unnamed x10, local copies, waits for them, and re-layouts  1.25 us
    dynamic_slice x2, local copies, waits for them, and re-layouts, shards(): lax.dynamic_slice_in_dim(v, odd, 1, 0)  0.97 us
  transfers between devices with their start and end apart: 5, of which 2 were waited for; matrix products, arithmetic and copies ran while one was open for 2% of the time, Pallas kernels for 35%

profile of v3, /device:TPU:1, one launch (start us, length us, event | category | flops | bytes accessed | tf_op | source)
XLA Modules:
  0.0 42.2 jit_solution(14785404149803452761)
XLA Ops:
  0.0 2.7 %collective-permute-start.2 = (f32[2,4,6,1,3312]{4,3,2,1,0:T(1,128)}, f32[2,4,6,1,3312]{4,3,2,1,0:T(1,128)S(1)}, u32[]{:S(2)}, u32[]{:S(2)}) collective-permute-start(f32[2,4,6,1,3312]{4,3,2,1,0:T(1,128)} %bitcast.4), channel_id=1, source_target_pairs={{0,1},{1,2},{2,3},{3,4},{4,5},{5,6},{6,7},{7,8},{8,9},{9,10},{10,1... | collective-permute-start | bytes 1907720 | tf_op jit(solution)/shard_map/ppermute | solution.py:386
  2.7 8.4 %first_layer.1 = (bf16[2,6,40,128]{3,2,1,0:T(8,128)(2,1)}, bf16[2,6,40,128]{3,2,1,0:T(8,128)(2,1)}) custom-call(bf16[6,12,8,192]{3,2,1,0:T(8,128)(2,1)} %bitcast.9, f32[2,2,192]{2,1,0:T(2,128)} %gains_ref.3, bf16[2,192,576]{2,1,0:T(8,128)(2,1)} %wqkv_any.1, bf16[2,192,192]{2,1,0:T(8,128)(2,1)} %wproj_any.1, bf16[2,192,768]{2,1,0:T(8,128)(2,1)} %wup_any.1, ...), custom_call_target="tpu_custom_call" | custom-call | tf_op jit(solution)/shard_map/first_layer/pallas_call | solution.py:397
  11.1 2.6 %collective-permute-start = (bf16[2,6,40,128]{3,2,1,0:T(8,128)(2,1)}, bf16[2,6,40,128]{3,2,1,0:T(8,128)(2,1)S(1)}, u32[]{:S(2)}, u32[]{:S(2)}) collective-permute-start(bf16[2,6,40,128]{3,2,1,0:T(8,128)(2,1)} %get-tuple-element.10.fast_any), channel_id=1, source_target_pairs={{0,16},{16,0},{32,48},{48,32},{64,80},{80,64},{96,112},{112,96},{1... | collective-permute-start | bytes 368648 | tf_op jit(solution)/shard_map/ppermute | solution.py:429
  13.8 5.6 %collective-permute-start.1 = (bf16[2,6,40,128]{3,2,1,0:T(8,128)(2,1)}, bf16[2,6,40,128]{3,2,1,0:T(8,128)(2,1)S(1)}, u32[]{:S(2)}, u32[]{:S(2)}) collective-permute-start(bf16[2,6,40,128]{3,2,1,0:T(8,128)(2,1)} %get-tuple-element.11.slow_any), channel_id=1, source_target_pairs={{0,240},{16,32},{32,16},{48,64},{64,48},{80,96},{96,80},{112,128},... | collective-permute-start | bytes 368648 | tf_op jit(solution)/shard_map/ppermute | solution.py:430
  19.4 0.9 %constant_dynamic-slice_fusion.2 = (bf16[1,6,40,128]{3,2,1,0:T(8,128)(2,1)S(1)}, bf16[1,6,40,128]{3,2,1,0:T(8,128)(2,1)S(1)}, bf16[1,6,40,128]{3,2,1,0:T(8,128)(2,1)S(1)}, bf16[1,6,40,128]{3,2,1,0:T(8,128)(2,1)S(1)}) fusion(bf16[2,6,40,128]{3,2,1,0:T(8,128)(2,1)} %get-tuple-element.11.slow_any, s32[]{:T(128)S(6)} %select_n.21, s32[]{:T(128)S(6)} %select_n.20, ...), kind=kLoop, calls=%fused_computation.4 | loop fusion | bytes 491528 | tf_op jit(solution)/shard_map/dynamic_slice | solution.py:443
  20.3 0.0 collective-permute-done.from_fast_any
  20.3 0.0 copy-start.1
  20.4 2.1 %collective-permute-done.1.from_slow_any = bf16[2,6,40,128]{3,2,1,0:T(8,128)(2,1)S(1)} collective-permute-done((bf16[2,6,40,128]{3,2,1,0:T(8,128)(2,1)}, bf16[2,6,40,128]{3,2,1,0:T(8,128)(2,1)S(1)}, u32[]{:S(2)}, u32[]{:S(2)}) %collective-permute-start.1) | collective-permute-done | bytes 122912 | tf_op jit(solution)/shard_map/ppermute | solution.py:430
  22.5 0.0 copy-start.2
  22.5 0.0 collective-permute-done.2.prev_tab_ref
  22.5 0.0 copy-start
  22.6 0.1 collective-permute-start.3
  22.7 1.9 %collective-permute-start.4 = (bf16[4,6,40,128]{3,2,1,0:T(8,128)(2,1)S(1)}, bf16[4,6,40,128]{3,2,1,0:T(8,128)(2,1)S(1)}, u32[]{:S(2)}, u32[]{:S(2)}) collective-permute-start(bf16[4,6,40,128]{3,2,1,0:T(8,128)(2,1)S(1)} %pad_maximum_fusion.1), channel_id=1, source_target_pairs={{0,15},{1,2},{2,1},{3,4},{4,3},{5,6},{6,5},{7,8},{8,7},{9,10},{10,... | collective-permute-start | bytes 737288 | tf_op jit(solution)/shard_map/ppermute | solution.py:445
  24.6 0.0 copy-done
  24.6 6.4 %second_bias.1.bias_any = bf16[16,240,160]{2,1,0:T(8,128)(2,1)} custom-call(f32[2,4,6,1,3312]{4,3,2,1,0:T(1,128)} %bitcast.6, f32[2,4,6,1,3312]{4,3,2,1,0:T(1,128)} %copy-done, f32[384,160]{1,0:T(8,128)} %constant.26.clone.select_ref), custom_call_target="tpu_custom_call" | custom-call | tf_op jit(solution)/shard_map/second_bias/pallas_call | solution.py:397
  31.1 0.0 copy-done.1
  31.1 0.0 copy-done.2
  31.1 0.0 collective-permute-done.3.lat_fast_any
  31.1 0.0 copy-start.3
  31.1 0.2 collective-permute-done.4.lat_slow_any
  31.3 0.5 %copy-done.3 = bf16[4,6,40,128]{3,2,1,0:T(8,128)(2,1)} copy-done((bf16[4,6,40,128]{3,2,1,0:T(8,128)(2,1)}, bf16[4,6,40,128]{3,2,1,0:T(8,128)(2,1)S(1)}, u32[]{:S(2)}) %copy-start.3) | copy-done | bytes 245784
  31.8 0.0 copy-start.4
  31.8 0.7 %copy-done.4 = bf16[4,6,40,128]{3,2,1,0:T(8,128)(2,1)} copy-done((bf16[4,6,40,128]{3,2,1,0:T(8,128)(2,1)}, bf16[4,6,40,128]{3,2,1,0:T(8,128)(2,1)S(1)}, u32[]{:S(2)}) %copy-start.4) | copy-done | bytes 245784
  32.5 9.6 %second_layer.1 = bf16[6,12,8,192]{3,2,1,0:T(8,128)(2,1)} custom-call(bf16[2,6,40,128]{3,2,1,0:T(8,128)(2,1)} %get-tuple-element.10.fast_any, bf16[2,6,40,128]{3,2,1,0:T(8,128)(2,1)} %get-tuple-element.11.slow_any, bf16[2,6,40,128]{3,2,1,0:T(8,128)(2,1)} %copy-done.1, bf16[2,6,40,128]{3,2,1,0:T(8,128)(2,1)} %copy-done.2, bf16[4,6,40,128]{3,2,1,0:T(8,128)(2,1)} %copy-done.3, ...), custom_call_target="tpu_custom_call" | custom-call | tf_op jit(solution)/shard_map/second_layer/pallas_call | solution.py:397
  (3 shorter events, 0.1 us)
Async XLA Ops:
  0.0 22.5 %collective-permute-start.2 = (f32[2,4,6,1,3312]{4,3,2,1,0:T(1,128)}, f32[2,4,6,1,3312]{4,3,2,1,0:T(1,128)S(1)}, u32[]{:S(2)}, u32[]{:S(2)}) collective-permute-start(f32[2,4,6,1,3312]{4,3,2,1,0:T(1,128)} %bitcast.4), channel_id=1, source_target_pairs={{0,1},{1,2},{2,3},{3,4},{4,5},{5,6},{6,7},{7,8},{8,9},{9,10},{10,1... | collective-permute-start | bytes 1907720 | tf_op jit(solution)/shard_map/ppermute | solution.py:386
  11.1 9.2 %collective-permute-start = (bf16[2,6,40,128]{3,2,1,0:T(8,128)(2,1)}, bf16[2,6,40,128]{3,2,1,0:T(8,128)(2,1)S(1)}, u32[]{:S(2)}, u32[]{:S(2)}) collective-permute-start(bf16[2,6,40,128]{3,2,1,0:T(8,128)(2,1)} %get-tuple-element.10.fast_any), channel_id=1, source_target_pairs={{0,16},{16,0},{32,48},{48,32},{64,80},{80,64},{96,112},{112,96},{1... | collective-permute-start | bytes 368648 | tf_op jit(solution)/shard_map/ppermute | solution.py:429
  13.8 8.7 %collective-permute-start.1 = (bf16[2,6,40,128]{3,2,1,0:T(8,128)(2,1)}, bf16[2,6,40,128]{3,2,1,0:T(8,128)(2,1)S(1)}, u32[]{:S(2)}, u32[]{:S(2)}) collective-permute-start(bf16[2,6,40,128]{3,2,1,0:T(8,128)(2,1)} %get-tuple-element.11.slow_any), channel_id=1, source_target_pairs={{0,240},{16,32},{32,16},{48,64},{64,48},{80,96},{96,80},{112,128},... | collective-permute-start | bytes 368648 | tf_op jit(solution)/shard_map/ppermute | solution.py:430
  20.3 10.7 %copy-start.1 = (bf16[2,6,40,128]{3,2,1,0:T(8,128)(2,1)}, bf16[2,6,40,128]{3,2,1,0:T(8,128)(2,1)S(1)}, u32[]{:S(2)}) copy-start(bf16[2,6,40,128]{3,2,1,0:T(8,128)(2,1)S(1)} %collective-permute-done.from_fast_any) | copy-start | bytes 368644
  22.5 8.6 %copy-start.2 = (bf16[2,6,40,128]{3,2,1,0:T(8,128)(2,1)}, bf16[2,6,40,128]{3,2,1,0:T(8,128)(2,1)S(1)}, u32[]{:S(2)}) copy-start(bf16[2,6,40,128]{3,2,1,0:T(8,128)(2,1)S(1)} %collective-permute-done.1.from_slow_any) | copy-start | bytes 368644
  22.5 2.1 %copy-start = (f32[2,4,6,1,3312]{4,3,2,1,0:T(1,128)}, f32[2,4,6,1,3312]{4,3,2,1,0:T(1,128)S(1)}, u32[]{:S(2)}) copy-start(f32[2,4,6,1,3312]{4,3,2,1,0:T(1,128)S(1)} %collective-permute-done.2.prev_tab_ref) | copy-start | bytes 1907716
  22.6 8.5 %collective-permute-start.3 = (bf16[4,6,40,128]{3,2,1,0:T(8,128)(2,1)S(1)}, bf16[4,6,40,128]{3,2,1,0:T(8,128)(2,1)S(1)}, u32[]{:S(2)}, u32[]{:S(2)}) collective-permute-start(bf16[4,6,40,128]{3,2,1,0:T(8,128)(2,1)S(1)} %pad_maximum_fusion), channel_id=1, source_target_pairs={{0,1},{1,0},{2,3},{3,2},{4,5},{5,4},{6,7},{7,6},{8,9},{9,8},{10,11... | collective-permute-start | bytes 737288 | tf_op jit(solution)/shard_map/ppermute | solution.py:444
  22.7 8.5 %collective-permute-start.4 = (bf16[4,6,40,128]{3,2,1,0:T(8,128)(2,1)S(1)}, bf16[4,6,40,128]{3,2,1,0:T(8,128)(2,1)S(1)}, u32[]{:S(2)}, u32[]{:S(2)}) collective-permute-start(bf16[4,6,40,128]{3,2,1,0:T(8,128)(2,1)S(1)} %pad_maximum_fusion.1), channel_id=1, source_target_pairs={{0,15},{1,2},{2,1},{3,4},{4,3},{5,6},{6,5},{7,8},{8,7},{9,10},{10,... | collective-permute-start | bytes 737288 | tf_op jit(solution)/shard_map/ppermute | solution.py:445
  31.1 0.7 %copy-start.3 = (bf16[4,6,40,128]{3,2,1,0:T(8,128)(2,1)}, bf16[4,6,40,128]{3,2,1,0:T(8,128)(2,1)S(1)}, u32[]{:S(2)}) copy-start(bf16[4,6,40,128]{3,2,1,0:T(8,128)(2,1)S(1)} %collective-permute-done.3.lat_fast_any) | copy-start | bytes 737284
  31.8 0.7 %copy-start.4 = (bf16[4,6,40,128]{3,2,1,0:T(8,128)(2,1)}, bf16[4,6,40,128]{3,2,1,0:T(8,128)(2,1)S(1)}, u32[]{:S(2)}) copy-start(bf16[4,6,40,128]{3,2,1,0:T(8,128)(2,1)S(1)} %collective-permute-done.4.lat_slow_any) | copy-start | bytes 737284

commit v4 on v3

--- a/solution.py
+++ b/solution.py
@@ -279,6 +279,32 @@
                 bias_ref[(b * 2 + a) * 4 + zw] = dot(wide.astype(BF16), select).astype(BF16)
 
 
+def holed(value, axis):
+    blank = jnp.zeros((value.shape[0], 64) if axis else (64, value.shape[1]), value.dtype)
+    head, last = (value[:, :128], value[:, 128:]) if axis else (value[:128], value[128:])
+    return (
+        jnp.concatenate([head, last, blank], axis=axis),
+        jnp.concatenate([head, blank, last], axis=axis),
+    )
+
+
+def holed_normalize(sources, zw, gain):
+    pair, second = divmod(zw, 2)
+    values = jnp.concatenate(
+        [
+            jnp.concatenate([src[pair * 3 + second], src[pair * 3 + 2]], axis=1).astype(F32)
+            for src in sources
+        ],
+        axis=0,
+    )
+    lanes = lax.broadcasted_iota(jnp.int32, (1, 256), 1)
+    there = (lanes < 128) | (lanes >= 192) if second else lanes < C
+    mean = jnp.sum(jnp.where(there, values, 0.0), axis=-1, keepdims=True) * (1.0 / C)
+    centered = jnp.where(there, values - mean, 0.0)
+    var = jnp.sum(centered * centered, axis=-1, keepdims=True) * (1.0 / C)
+    return (centered * lax.rsqrt(var + EPS) * gain).astype(BF16)
+
+
 def second_kernel(
     fast_any, slow_any, from_fast_any, from_slow_any, lat_fast_any, lat_slow_any, bias_any,
     gains_ref, wqkv_any, wproj_any, wup_any, wdown_any,
@@ -308,8 +334,9 @@
     gain_two = gains_ref[1, 1:2]
     fetch.wait("near0", "near1", "qkv")
     wq = qkv_ref[:, :C]
-    wk = qkv_ref[:, C : 2 * C]
-    wv = value_weights(qkv_ref)
+    wk = holed(qkv_ref[:, C : 2 * C], 0)
+    wv = holed(value_weights(qkv_ref), 0)
+    gains = holed(gain_one, 1)
     for b in range(2):
         for a in range(2):
             for zw in range(4):
@@ -328,10 +355,9 @@
             items = []
             for zw in range(4):
                 chunk = (b * 2 + a) * 4 + zw
-                tokens = jnp.concatenate([block_of(src, zw) for src in sources], axis=0)
-                normed = normalize(tokens, gain_one)
-                keys = dot(normed, wk).astype(BF16)
-                values = with_ones(dot(normed, wv))
+                normed = holed_normalize(sources, zw, gains[zw % 2])
+                keys = dot(normed, wk[zw % 2]).astype(BF16)
+                values = with_ones(dot(normed, wv[zw % 2]))
                 items.append(
                     (keys, values, query[chunk * QP : (chunk + 1) * QP],
                      lambda chunk=chunk: bias_ref[chunk].astype(F32))

time: 42.5 us -> 41.2 us (0.969)
  Pallas kernels: 24.4 us -> 23.1 us
    pallas_call x3, Pallas kernels: 24.4 us -> 23.1 us  [call(): pl.pallas_call(kernel, grid=(1,), in_specs=in_specs, out_specs=specs[0] i...]
  transfers between devices with their start and end apart: 5 -> 5, of which waited for: 2 -> 2; matrix products, arithmetic and copies ran while one was open for 2% -> 2% of each run, Pallas kernels for 35% -> 36%
where the time goes in v4:
time: 41.2 us; the launch traced here: 40.9 us
  Pallas kernels  23.1 us (56%)
  starting transfers between devices  13 us (32%)
  waiting for transfers between devices  2.3 us (6%)
  local copies, waits for them, and re-layouts  2.22 us (5%)
    pallas_call x3, Pallas kernels, call(): pl.pallas_call(kernel, grid=(1,), in_specs=in_specs, out_specs=specs[0] i...  23.1 us
    ppermute x1, starting transfers between devices, shards(): from_slow = lax.ppermute(slow, 'lon', paired('lon', 1))  5.63 us
    ppermute x1, starting transfers between devices, shifted(): return lax.ppermute(value, axis, pairs)  2.69 us
    ppermute x1, starting transfers between devices, shards(): from_fast = lax.ppermute(fast, 'lon', paired('lon', 0))  2.63 us
    ppermute x1, waiting for transfers between devices, shards(): from_slow = lax.ppermute(slow, 'lon', paired('lon', 1))  2.13 us
    ppermute x1, starting transfers between devices, shards(): lat_slow = lax.ppermute(toward_slow, 'lat', paired('lat', 1))  1.91 us
    unnamed x10, local copies, waits for them, and re-layouts  1.25 us
    dynamic_slice x2, local copies, waits for them, and re-layouts, shards(): lax.dynamic_slice_in_dim(v, odd, 1, 0)  0.97 us
  transfers between devices with their start and end apart: 5, of which 2 were waited for; matrix products, arithmetic and copies ran while one was open for 2% of the time, Pallas kernels for 36%

profile of v4, /device:TPU:1, one launch (start us, length us, event | category | flops | bytes accessed | tf_op | source)
XLA Modules:
  0.0 40.9 jit_solution(16817655404748873789)
XLA Ops:
  0.0 2.7 %collective-permute-start.2 = (f32[2,4,6,1,3312]{4,3,2,1,0:T(1,128)}, f32[2,4,6,1,3312]{4,3,2,1,0:T(1,128)S(1)}, u32[]{:S(2)}, u32[]{:S(2)}) collective-permute-start(f32[2,4,6,1,3312]{4,3,2,1,0:T(1,128)} %bitcast.4), channel_id=1, source_target_pairs={{0,1},{1,2},{2,3},{3,4},{4,5},{5,6},{6,7},{7,8},{8,9},{9,10},{10,1... | collective-permute-start | bytes 1907720 | tf_op jit(solution)/shard_map/ppermute | solution.py:412
  2.7 8.4 %first_layer.1 = (bf16[2,6,40,128]{3,2,1,0:T(8,128)(2,1)}, bf16[2,6,40,128]{3,2,1,0:T(8,128)(2,1)}) custom-call(bf16[6,12,8,192]{3,2,1,0:T(8,128)(2,1)} %bitcast.9, f32[2,2,192]{2,1,0:T(2,128)} %gains_ref.3, bf16[2,192,576]{2,1,0:T(8,128)(2,1)} %wqkv_any.1, bf16[2,192,192]{2,1,0:T(8,128)(2,1)} %wproj_any.1, bf16[2,192,768]{2,1,0:T(8,128)(2,1)} %wup_any.1, ...), custom_call_target="tpu_custom_call" | custom-call | tf_op jit(solution)/shard_map/first_layer/pallas_call | solution.py:423
  11.1 2.6 %collective-permute-start = (bf16[2,6,40,128]{3,2,1,0:T(8,128)(2,1)}, bf16[2,6,40,128]{3,2,1,0:T(8,128)(2,1)S(1)}, u32[]{:S(2)}, u32[]{:S(2)}) collective-permute-start(bf16[2,6,40,128]{3,2,1,0:T(8,128)(2,1)} %get-tuple-element.10.fast_any), channel_id=1, source_target_pairs={{0,16},{16,0},{32,48},{48,32},{64,80},{80,64},{96,112},{112,96},{1... | collective-permute-start | bytes 368648 | tf_op jit(solution)/shard_map/ppermute | solution.py:455
  13.8 5.6 %collective-permute-start.1 = (bf16[2,6,40,128]{3,2,1,0:T(8,128)(2,1)}, bf16[2,6,40,128]{3,2,1,0:T(8,128)(2,1)S(1)}, u32[]{:S(2)}, u32[]{:S(2)}) collective-permute-start(bf16[2,6,40,128]{3,2,1,0:T(8,128)(2,1)} %get-tuple-element.11.slow_any), channel_id=1, source_target_pairs={{0,240},{16,32},{32,16},{48,64},{64,48},{80,96},{96,80},{112,128},... | collective-permute-start | bytes 368648 | tf_op jit(solution)/shard_map/ppermute | solution.py:456
  19.4 0.9 %constant_dynamic-slice_fusion.2 = (bf16[1,6,40,128]{3,2,1,0:T(8,128)(2,1)S(1)}, bf16[1,6,40,128]{3,2,1,0:T(8,128)(2,1)S(1)}, bf16[1,6,40,128]{3,2,1,0:T(8,128)(2,1)S(1)}, bf16[1,6,40,128]{3,2,1,0:T(8,128)(2,1)S(1)}) fusion(bf16[2,6,40,128]{3,2,1,0:T(8,128)(2,1)} %get-tuple-element.11.slow_any, s32[]{:T(128)S(6)} %select_n.21, s32[]{:T(128)S(6)} %select_n.20, ...), kind=kLoop, calls=%fused_computation.4 | loop fusion | bytes 491528 | tf_op jit(solution)/shard_map/dynamic_slice | solution.py:469
  20.3 0.0 collective-permute-done.from_fast_any
  20.3 0.0 copy-start.1
  20.4 2.1 %collective-permute-done.1.from_slow_any = bf16[2,6,40,128]{3,2,1,0:T(8,128)(2,1)S(1)} collective-permute-done((bf16[2,6,40,128]{3,2,1,0:T(8,128)(2,1)}, bf16[2,6,40,128]{3,2,1,0:T(8,128)(2,1)S(1)}, u32[]{:S(2)}, u32[]{:S(2)}) %collective-permute-start.1) | collective-permute-done | bytes 122912 | tf_op jit(solution)/shard_map/ppermute | solution.py:456
  22.5 0.0 copy-start.2
  22.5 0.0 collective-permute-done.2.prev_tab_ref
  22.5 0.0 copy-start
  22.6 0.1 collective-permute-start.3
  22.7 1.9 %collective-permute-start.4 = (bf16[4,6,40,128]{3,2,1,0:T(8,128)(2,1)S(1)}, bf16[4,6,40,128]{3,2,1,0:T(8,128)(2,1)S(1)}, u32[]{:S(2)}, u32[]{:S(2)}) collective-permute-start(bf16[4,6,40,128]{3,2,1,0:T(8,128)(2,1)S(1)} %pad_maximum_fusion.1), channel_id=1, source_target_pairs={{0,15},{1,2},{2,1},{3,4},{4,3},{5,6},{6,5},{7,8},{8,7},{9,10},{10,... | collective-permute-start | bytes 737288 | tf_op jit(solution)/shard_map/ppermute | solution.py:471
  24.6 0.0 copy-done
  24.6 6.4 %second_bias.1.bias_any = bf16[16,240,160]{2,1,0:T(8,128)(2,1)} custom-call(f32[2,4,6,1,3312]{4,3,2,1,0:T(1,128)} %bitcast.6, f32[2,4,6,1,3312]{4,3,2,1,0:T(1,128)} %copy-done, f32[384,160]{1,0:T(8,128)} %constant.26.clone.select_ref), custom_call_target="tpu_custom_call" | custom-call | tf_op jit(solution)/shard_map/second_bias/pallas_call | solution.py:423
  31.1 0.0 copy-done.1
  31.1 0.0 copy-done.2
  31.1 0.0 collective-permute-done.3.lat_fast_any
  31.1 0.0 copy-start.3
  31.1 0.2 collective-permute-done.4.lat_slow_any
  31.3 0.5 %copy-done.3 = bf16[4,6,40,128]{3,2,1,0:T(8,128)(2,1)} copy-done((bf16[4,6,40,128]{3,2,1,0:T(8,128)(2,1)}, bf16[4,6,40,128]{3,2,1,0:T(8,128)(2,1)S(1)}, u32[]{:S(2)}) %copy-start.3) | copy-done | bytes 245784
  31.8 0.0 copy-start.4
  31.8 0.7 %copy-done.4 = bf16[4,6,40,128]{3,2,1,0:T(8,128)(2,1)} copy-done((bf16[4,6,40,128]{3,2,1,0:T(8,128)(2,1)}, bf16[4,6,40,128]{3,2,1,0:T(8,128)(2,1)S(1)}, u32[]{:S(2)}) %copy-start.4) | copy-done | bytes 245784
  32.5 8.2 %second_layer.1 = bf16[6,12,8,192]{3,2,1,0:T(8,128)(2,1)} custom-call(bf16[2,6,40,128]{3,2,1,0:T(8,128)(2,1)} %get-tuple-element.10.fast_any, bf16[2,6,40,128]{3,2,1,0:T(8,128)(2,1)} %get-tuple-element.11.slow_any, bf16[2,6,40,128]{3,2,1,0:T(8,128)(2,1)} %copy-done.1, bf16[2,6,40,128]{3,2,1,0:T(8,128)(2,1)} %copy-done.2, bf16[4,6,40,128]{3,2,1,0:T(8,128)(2,1)} %copy-done.3, ...), custom_call_target="tpu_custom_call" | custom-call | tf_op jit(solution)/shard_map/second_layer/pallas_call | solution.py:423
  (3 shorter events, 0.1 us)
Async XLA Ops:
  0.0 22.5 %collective-permute-start.2 = (f32[2,4,6,1,3312]{4,3,2,1,0:T(1,128)}, f32[2,4,6,1,3312]{4,3,2,1,0:T(1,128)S(1)}, u32[]{:S(2)}, u32[]{:S(2)}) collective-permute-start(f32[2,4,6,1,3312]{4,3,2,1,0:T(1,128)} %bitcast.4), channel_id=1, source_target_pairs={{0,1},{1,2},{2,3},{3,4},{4,5},{5,6},{6,7},{7,8},{8,9},{9,10},{10,1... | collective-permute-start | bytes 1907720 | tf_op jit(solution)/shard_map/ppermute | solution.py:412
  11.1 9.2 %collective-permute-start = (bf16[2,6,40,128]{3,2,1,0:T(8,128)(2,1)}, bf16[2,6,40,128]{3,2,1,0:T(8,128)(2,1)S(1)}, u32[]{:S(2)}, u32[]{:S(2)}) collective-permute-start(bf16[2,6,40,128]{3,2,1,0:T(8,128)(2,1)} %get-tuple-element.10.fast_any), channel_id=1, source_target_pairs={{0,16},{16,0},{32,48},{48,32},{64,80},{80,64},{96,112},{112,96},{1... | collective-permute-start | bytes 368648 | tf_op jit(solution)/shard_map/ppermute | solution.py:455
  13.8 8.7 %collective-permute-start.1 = (bf16[2,6,40,128]{3,2,1,0:T(8,128)(2,1)}, bf16[2,6,40,128]{3,2,1,0:T(8,128)(2,1)S(1)}, u32[]{:S(2)}, u32[]{:S(2)}) collective-permute-start(bf16[2,6,40,128]{3,2,1,0:T(8,128)(2,1)} %get-tuple-element.11.slow_any), channel_id=1, source_target_pairs={{0,240},{16,32},{32,16},{48,64},{64,48},{80,96},{96,80},{112,128},... | collective-permute-start | bytes 368648 | tf_op jit(solution)/shard_map/ppermute | solution.py:456
  20.3 10.7 %copy-start.1 = (bf16[2,6,40,128]{3,2,1,0:T(8,128)(2,1)}, bf16[2,6,40,128]{3,2,1,0:T(8,128)(2,1)S(1)}, u32[]{:S(2)}) copy-start(bf16[2,6,40,128]{3,2,1,0:T(8,128)(2,1)S(1)} %collective-permute-done.from_fast_any) | copy-start | bytes 368644
  22.5 8.6 %copy-start.2 = (bf16[2,6,40,128]{3,2,1,0:T(8,128)(2,1)}, bf16[2,6,40,128]{3,2,1,0:T(8,128)(2,1)S(1)}, u32[]{:S(2)}) copy-start(bf16[2,6,40,128]{3,2,1,0:T(8,128)(2,1)S(1)} %collective-permute-done.1.from_slow_any) | copy-start | bytes 368644
  22.5 2.1 %copy-start = (f32[2,4,6,1,3312]{4,3,2,1,0:T(1,128)}, f32[2,4,6,1,3312]{4,3,2,1,0:T(1,128)S(1)}, u32[]{:S(2)}) copy-start(f32[2,4,6,1,3312]{4,3,2,1,0:T(1,128)S(1)} %collective-permute-done.2.prev_tab_ref) | copy-start | bytes 1907716
  22.6 8.5 %collective-permute-start.3 = (bf16[4,6,40,128]{3,2,1,0:T(8,128)(2,1)S(1)}, bf16[4,6,40,128]{3,2,1,0:T(8,128)(2,1)S(1)}, u32[]{:S(2)}, u32[]{:S(2)}) collective-permute-start(bf16[4,6,40,128]{3,2,1,0:T(8,128)(2,1)S(1)} %pad_maximum_fusion), channel_id=1, source_target_pairs={{0,1},{1,0},{2,3},{3,2},{4,5},{5,4},{6,7},{7,6},{8,9},{9,8},{10,11... | collective-permute-start | bytes 737288 | tf_op jit(solution)/shard_map/ppermute | solution.py:470
  22.7 8.5 %collective-permute-start.4 = (bf16[4,6,40,128]{3,2,1,0:T(8,128)(2,1)S(1)}, bf16[4,6,40,128]{3,2,1,0:T(8,128)(2,1)S(1)}, u32[]{:S(2)}, u32[]{:S(2)}) collective-permute-start(bf16[4,6,40,128]{3,2,1,0:T(8,128)(2,1)S(1)} %pad_maximum_fusion.1), channel_id=1, source_target_pairs={{0,15},{1,2},{2,1},{3,4},{4,3},{5,6},{6,5},{7,8},{8,7},{9,10},{10,... | collective-permute-start | bytes 737288 | tf_op jit(solution)/shard_map/ppermute | solution.py:471
  31.1 0.7 %copy-start.3 = (bf16[4,6,40,128]{3,2,1,0:T(8,128)(2,1)}, bf16[4,6,40,128]{3,2,1,0:T(8,128)(2,1)S(1)}, u32[]{:S(2)}) copy-start(bf16[4,6,40,128]{3,2,1,0:T(8,128)(2,1)S(1)} %collective-permute-done.3.lat_fast_any) | copy-start | bytes 737284
  31.8 0.7 %copy-start.4 = (bf16[4,6,40,128]{3,2,1,0:T(8,128)(2,1)}, bf16[4,6,40,128]{3,2,1,0:T(8,128)(2,1)S(1)}, u32[]{:S(2)}) copy-start(bf16[4,6,40,128]{3,2,1,0:T(8,128)(2,1)S(1)} %collective-permute-done.4.lat_slow_any) | copy-start | bytes 737284

commit v5 on v4

--- a/solution.py
+++ b/solution.py
@@ -343,7 +343,7 @@
                 at = ((b * 2 + a) * 4 + zw) * QP
                 own_ref[at : at + QP, :] = block_of(near_ref.at[1 + b, a], zw)
     query = dot(normalize(own_ref[...], gain_one), wq) * QSCALE
-    fetch.wait("near2", "near3", "bias")
+    fetch.wait("near2", "near3")
     fetch.wait(*[f"{kind}{i}" for kind in ("fast", "slow") for i in range(4)])
     above = [vert_ref.at[0, i] for i in range(4)]
     here = [[near_ref.at[i, a] for i in range(4)] for a in range(2)]
@@ -362,6 +362,8 @@
                     (keys, values, query[chunk * QP : (chunk + 1) * QP],
                      lambda chunk=chunk: bias_ref[chunk].astype(F32))
                 )
+            if a == b == 0:
+                fetch.wait("bias")
             for zw, out in enumerate(attend(items)):
                 chunk = (b * 2 + a) * 4 + zw
                 o_ref[chunk * QP : (chunk + 1) * QP, :] = out

time: 41.2 us -> 41 us (level)
  no operation moved by 1% of the time
where the time goes in v5:
time: 41 us; the launch traced here: 40.8 us
  Pallas kernels  23 us (56%)
  starting transfers between devices  13 us (32%)
  waiting for transfers between devices  2.3 us (6%)
  local copies, waits for them, and re-layouts  2.22 us (5%)
    pallas_call x3, Pallas kernels, call(): pl.pallas_call(kernel, grid=(1,), in_specs=in_specs, out_specs=specs[0] i...  23 us
    ppermute x1, starting transfers between devices, shards(): from_slow = lax.ppermute(slow, 'lon', paired('lon', 1))  5.63 us
    ppermute x1, starting transfers between devices, shifted(): return lax.ppermute(value, axis, pairs)  2.69 us
    ppermute x1, starting transfers between devices, shards(): from_fast = lax.ppermute(fast, 'lon', paired('lon', 0))  2.63 us
    ppermute x1, waiting for transfers between devices, shards(): from_slow = lax.ppermute(slow, 'lon', paired('lon', 1))  2.13 us
    ppermute x1, starting transfers between devices, shards(): lat_slow = lax.ppermute(toward_slow, 'lat', paired('lat', 1))  1.91 us
    unnamed x10, local copies, waits for them, and re-layouts  1.25 us
    dynamic_slice x2, local copies, waits for them, and re-layouts, shards(): lax.dynamic_slice_in_dim(v, odd, 1, 0)  0.97 us
  transfers between devices with their start and end apart: 5, of which 2 were waited for; matrix products, arithmetic and copies ran while one was open for 2% of the time, Pallas kernels for 36%

profile of v5, /device:TPU:1, one launch (start us, length us, event | category | flops | bytes accessed | tf_op | source)
XLA Modules:
  0.0 40.8 jit_solution(14161197152270201095)
XLA Ops:
  0.0 2.7 %collective-permute-start.2 = (f32[2,4,6,1,3312]{4,3,2,1,0:T(1,128)}, f32[2,4,6,1,3312]{4,3,2,1,0:T(1,128)S(1)}, u32[]{:S(2)}, u32[]{:S(2)}) collective-permute-start(f32[2,4,6,1,3312]{4,3,2,1,0:T(1,128)} %bitcast.4), channel_id=1, source_target_pairs={{0,1},{1,2},{2,3},{3,4},{4,5},{5,6},{6,7},{7,8},{8,9},{9,10},{10,1... | collective-permute-start | bytes 1907720 | tf_op jit(solution)/shard_map/ppermute | solution.py:414
  2.7 8.4 %first_layer.1 = (bf16[2,6,40,128]{3,2,1,0:T(8,128)(2,1)}, bf16[2,6,40,128]{3,2,1,0:T(8,128)(2,1)}) custom-call(bf16[6,12,8,192]{3,2,1,0:T(8,128)(2,1)} %bitcast.9, f32[2,2,192]{2,1,0:T(2,128)} %gains_ref.3, bf16[2,192,576]{2,1,0:T(8,128)(2,1)} %wqkv_any.1, bf16[2,192,192]{2,1,0:T(8,128)(2,1)} %wproj_any.1, bf16[2,192,768]{2,1,0:T(8,128)(2,1)} %wup_any.1, ...), custom_call_target="tpu_custom_call" | custom-call | tf_op jit(solution)/shard_map/first_layer/pallas_call | solution.py:425
  11.1 2.6 %collective-permute-start = (bf16[2,6,40,128]{3,2,1,0:T(8,128)(2,1)}, bf16[2,6,40,128]{3,2,1,0:T(8,128)(2,1)S(1)}, u32[]{:S(2)}, u32[]{:S(2)}) collective-permute-start(bf16[2,6,40,128]{3,2,1,0:T(8,128)(2,1)} %get-tuple-element.10.fast_any), channel_id=1, source_target_pairs={{0,16},{16,0},{32,48},{48,32},{64,80},{80,64},{96,112},{112,96},{1... | collective-permute-start | bytes 368648 | tf_op jit(solution)/shard_map/ppermute | solution.py:457
  13.8 5.6 %collective-permute-start.1 = (bf16[2,6,40,128]{3,2,1,0:T(8,128)(2,1)}, bf16[2,6,40,128]{3,2,1,0:T(8,128)(2,1)S(1)}, u32[]{:S(2)}, u32[]{:S(2)}) collective-permute-start(bf16[2,6,40,128]{3,2,1,0:T(8,128)(2,1)} %get-tuple-element.11.slow_any), channel_id=1, source_target_pairs={{0,240},{16,32},{32,16},{48,64},{64,48},{80,96},{96,80},{112,128},... | collective-permute-start | bytes 368648 | tf_op jit(solution)/shard_map/ppermute | solution.py:458
  19.4 0.9 %constant_dynamic-slice_fusion.2 = (bf16[1,6,40,128]{3,2,1,0:T(8,128)(2,1)S(1)}, bf16[1,6,40,128]{3,2,1,0:T(8,128)(2,1)S(1)}, bf16[1,6,40,128]{3,2,1,0:T(8,128)(2,1)S(1)}, bf16[1,6,40,128]{3,2,1,0:T(8,128)(2,1)S(1)}) fusion(bf16[2,6,40,128]{3,2,1,0:T(8,128)(2,1)} %get-tuple-element.11.slow_any, s32[]{:T(128)S(6)} %select_n.21, s32[]{:T(128)S(6)} %select_n.20, ...), kind=kLoop, calls=%fused_computation.4 | loop fusion | bytes 491528 | tf_op jit(solution)/shard_map/dynamic_slice | solution.py:471
  20.3 0.0 collective-permute-done.from_fast_any
  20.3 0.0 copy-start.1
  20.4 2.1 %collective-permute-done.1.from_slow_any = bf16[2,6,40,128]{3,2,1,0:T(8,128)(2,1)S(1)} collective-permute-done((bf16[2,6,40,128]{3,2,1,0:T(8,128)(2,1)}, bf16[2,6,40,128]{3,2,1,0:T(8,128)(2,1)S(1)}, u32[]{:S(2)}, u32[]{:S(2)}) %collective-permute-start.1) | collective-permute-done | bytes 122912 | tf_op jit(solution)/shard_map/ppermute | solution.py:458
  22.5 0.0 copy-start.2
  22.5 0.0 collective-permute-done.2.prev_tab_ref
  22.5 0.0 copy-start
  22.6 0.1 collective-permute-start.3
  22.7 1.9 %collective-permute-start.4 = (bf16[4,6,40,128]{3,2,1,0:T(8,128)(2,1)S(1)}, bf16[4,6,40,128]{3,2,1,0:T(8,128)(2,1)S(1)}, u32[]{:S(2)}, u32[]{:S(2)}) collective-permute-start(bf16[4,6,40,128]{3,2,1,0:T(8,128)(2,1)S(1)} %pad_maximum_fusion.1), channel_id=1, source_target_pairs={{0,15},{1,2},{2,1},{3,4},{4,3},{5,6},{6,5},{7,8},{8,7},{9,10},{10,... | collective-permute-start | bytes 737288 | tf_op jit(solution)/shard_map/ppermute | solution.py:473
  24.6 0.0 copy-done
  24.6 6.4 %second_bias.1.bias_any = bf16[16,240,160]{2,1,0:T(8,128)(2,1)} custom-call(f32[2,4,6,1,3312]{4,3,2,1,0:T(1,128)} %bitcast.6, f32[2,4,6,1,3312]{4,3,2,1,0:T(1,128)} %copy-done, f32[384,160]{1,0:T(8,128)} %constant.26.clone.select_ref), custom_call_target="tpu_custom_call" | custom-call | tf_op jit(solution)/shard_map/second_bias/pallas_call | solution.py:425
  31.1 0.0 copy-done.1
  31.1 0.0 copy-done.2
  31.1 0.0 collective-permute-done.3.lat_fast_any
  31.1 0.0 copy-start.3
  31.1 0.2 collective-permute-done.4.lat_slow_any
  31.3 0.5 %copy-done.3 = bf16[4,6,40,128]{3,2,1,0:T(8,128)(2,1)} copy-done((bf16[4,6,40,128]{3,2,1,0:T(8,128)(2,1)}, bf16[4,6,40,128]{3,2,1,0:T(8,128)(2,1)S(1)}, u32[]{:S(2)}) %copy-start.3) | copy-done | bytes 245784
  31.8 0.0 copy-start.4
  31.8 0.7 %copy-done.4 = bf16[4,6,40,128]{3,2,1,0:T(8,128)(2,1)} copy-done((bf16[4,6,40,128]{3,2,1,0:T(8,128)(2,1)}, bf16[4,6,40,128]{3,2,1,0:T(8,128)(2,1)S(1)}, u32[]{:S(2)}) %copy-start.4) | copy-done | bytes 245784
  32.5 8.1 %second_layer.1 = bf16[6,12,8,192]{3,2,1,0:T(8,128)(2,1)} custom-call(bf16[2,6,40,128]{3,2,1,0:T(8,128)(2,1)} %get-tuple-element.10.fast_any, bf16[2,6,40,128]{3,2,1,0:T(8,128)(2,1)} %get-tuple-element.11.slow_any, bf16[2,6,40,128]{3,2,1,0:T(8,128)(2,1)} %copy-done.1, bf16[2,6,40,128]{3,2,1,0:T(8,128)(2,1)} %copy-done.2, bf16[4,6,40,128]{3,2,1,0:T(8,128)(2,1)} %copy-done.3, ...), custom_call_target="tpu_custom_call" | custom-call | tf_op jit(solution)/shard_map/second_layer/pallas_call | solution.py:425
  (3 shorter events, 0.1 us)
Async XLA Ops:
  0.0 22.5 %collective-permute-start.2 = (f32[2,4,6,1,3312]{4,3,2,1,0:T(1,128)}, f32[2,4,6,1,3312]{4,3,2,1,0:T(1,128)S(1)}, u32[]{:S(2)}, u32[]{:S(2)}) collective-permute-start(f32[2,4,6,1,3312]{4,3,2,1,0:T(1,128)} %bitcast.4), channel_id=1, source_target_pairs={{0,1},{1,2},{2,3},{3,4},{4,5},{5,6},{6,7},{7,8},{8,9},{9,10},{10,1... | collective-permute-start | bytes 1907720 | tf_op jit(solution)/shard_map/ppermute | solution.py:414
  11.1 9.2 %collective-permute-start = (bf16[2,6,40,128]{3,2,1,0:T(8,128)(2,1)}, bf16[2,6,40,128]{3,2,1,0:T(8,128)(2,1)S(1)}, u32[]{:S(2)}, u32[]{:S(2)}) collective-permute-start(bf16[2,6,40,128]{3,2,1,0:T(8,128)(2,1)} %get-tuple-element.10.fast_any), channel_id=1, source_target_pairs={{0,16},{16,0},{32,48},{48,32},{64,80},{80,64},{96,112},{112,96},{1... | collective-permute-start | bytes 368648 | tf_op jit(solution)/shard_map/ppermute | solution.py:457
  13.8 8.7 %collective-permute-start.1 = (bf16[2,6,40,128]{3,2,1,0:T(8,128)(2,1)}, bf16[2,6,40,128]{3,2,1,0:T(8,128)(2,1)S(1)}, u32[]{:S(2)}, u32[]{:S(2)}) collective-permute-start(bf16[2,6,40,128]{3,2,1,0:T(8,128)(2,1)} %get-tuple-element.11.slow_any), channel_id=1, source_target_pairs={{0,240},{16,32},{32,16},{48,64},{64,48},{80,96},{96,80},{112,128},... | collective-permute-start | bytes 368648 | tf_op jit(solution)/shard_map/ppermute | solution.py:458
  20.3 10.7 %copy-start.1 = (bf16[2,6,40,128]{3,2,1,0:T(8,128)(2,1)}, bf16[2,6,40,128]{3,2,1,0:T(8,128)(2,1)S(1)}, u32[]{:S(2)}) copy-start(bf16[2,6,40,128]{3,2,1,0:T(8,128)(2,1)S(1)} %collective-permute-done.from_fast_any) | copy-start | bytes 368644
  22.5 8.6 %copy-start.2 = (bf16[2,6,40,128]{3,2,1,0:T(8,128)(2,1)}, bf16[2,6,40,128]{3,2,1,0:T(8,128)(2,1)S(1)}, u32[]{:S(2)}) copy-start(bf16[2,6,40,128]{3,2,1,0:T(8,128)(2,1)S(1)} %collective-permute-done.1.from_slow_any) | copy-start | bytes 368644
  22.5 2.1 %copy-start = (f32[2,4,6,1,3312]{4,3,2,1,0:T(1,128)}, f32[2,4,6,1,3312]{4,3,2,1,0:T(1,128)S(1)}, u32[]{:S(2)}) copy-start(f32[2,4,6,1,3312]{4,3,2,1,0:T(1,128)S(1)} %collective-permute-done.2.prev_tab_ref) | copy-start | bytes 1907716
  22.6 8.5 %collective-permute-start.3 = (bf16[4,6,40,128]{3,2,1,0:T(8,128)(2,1)S(1)}, bf16[4,6,40,128]{3,2,1,0:T(8,128)(2,1)S(1)}, u32[]{:S(2)}, u32[]{:S(2)}) collective-permute-start(bf16[4,6,40,128]{3,2,1,0:T(8,128)(2,1)S(1)} %pad_maximum_fusion), channel_id=1, source_target_pairs={{0,1},{1,0},{2,3},{3,2},{4,5},{5,4},{6,7},{7,6},{8,9},{9,8},{10,11... | collective-permute-start | bytes 737288 | tf_op jit(solution)/shard_map/ppermute | solution.py:472
  22.7 8.5 %collective-permute-start.4 = (bf16[4,6,40,128]{3,2,1,0:T(8,128)(2,1)S(1)}, bf16[4,6,40,128]{3,2,1,0:T(8,128)(2,1)S(1)}, u32[]{:S(2)}, u32[]{:S(2)}) collective-permute-start(bf16[4,6,40,128]{3,2,1,0:T(8,128)(2,1)S(1)} %pad_maximum_fusion.1), channel_id=1, source_target_pairs={{0,15},{1,2},{2,1},{3,4},{4,3},{5,6},{6,5},{7,8},{8,7},{9,10},{10,... | collective-permute-start | bytes 737288 | tf_op jit(solution)/shard_map/ppermute | solution.py:473
  31.1 0.7 %copy-start.3 = (bf16[4,6,40,128]{3,2,1,0:T(8,128)(2,1)}, bf16[4,6,40,128]{3,2,1,0:T(8,128)(2,1)S(1)}, u32[]{:S(2)}) copy-start(bf16[4,6,40,128]{3,2,1,0:T(8,128)(2,1)S(1)} %collective-permute-done.3.lat_fast_any) | copy-start | bytes 737284
  31.8 0.7 %copy-start.4 = (bf16[4,6,40,128]{3,2,1,0:T(8,128)(2,1)}, bf16[4,6,40,128]{3,2,1,0:T(8,128)(2,1)S(1)}, u32[]{:S(2)}) copy-start(bf16[4,6,40,128]{3,2,1,0:T(8,128)(2,1)S(1)} %collective-permute-done.4.lat_slow_any) | copy-start | bytes 737284
